TPU v7x, 512 devices: a whole 4x4x16 slice. The times are simulated.
512 devices in a mesh: rows: 32 (over z, core), vocab: 16 (over x, y).
Axes of the slice: x: 4, y: 4, z: 16, core: 2. Of those that a mesh axis runs over, the one named last changes fastest.
Arguments:
- hidden: bfloat16 [1024, 5376], P('rows'), may hold values from -6 to 6
- logits: bfloat16 [1024, 131072], P(None, ('vocab', 'rows')), may hold values from -120 to 260
- eta: float32 [1024], replicated, may hold values from 0.0001 to 0.003
- teacher: int32 [1024], replicated, may hold values from 0 to 131071
- valid: int32 [1024], replicated, may hold values 0 or 1
Outputs:
- head_grad: bfloat16 [131072, 5376], P(('vocab', 'rows'))
- row_loss: float32 [1024], P(('rows', 'vocab'))
All inputs are finite; a program needn't handle non-finite values.
Results may differ from a plain program's by a relative error of at most 0.0028.
Values may be sent and summed in bfloat16 or wider, within the bound.
No kernel may reach another device: no remote copies, remote signals or barrier semaphores. Data moves between devices by JAX's collectives and lax.ppermute only.
A program may use at most 64 MiB of HBM per device.

v0:
```python
import jax
import jax.numpy as jnp
from jax import lax
from jax.sharding import PartitionSpec as P


def cutoff_terms(z, e, total, spread, columns, eta, teacher):
    entropy = jnp.log(total) - spread / total
    cutoff = jnp.minimum(eta, jnp.sqrt(eta) * jnp.exp(-entropy))
    chosen = columns[None, :] == teacher[:, None]
    kept = jnp.where((e > (cutoff * total)[:, None]) | chosen, e, jnp.float32(0.0))
    picked = jnp.where(chosen, z, jnp.float32(0.0))
    return (kept, chosen, jnp.sum(kept, axis=1), jnp.sum(picked, axis=1))


def finish(kept, chosen, mass, peak, target, live):
    grads = (live[:, None] * (kept / mass[:, None] - chosen.astype(jnp.float32))).astype(
        jnp.bfloat16
    )
    row_loss = live * (jnp.log(mass) + peak - target)
    return (grads, row_loss)


def per_device(hidden, logits, eta, teacher, valid):
    rows_dev = hidden.shape[0]
    n_vocab = lax.axis_size("vocab")
    share = rows_dev // n_vocab
    whole = lax.all_gather(hidden, "rows", axis=0, tiled=True)
    first = (lax.axis_index("rows") * n_vocab + lax.axis_index("vocab")) * share
    live_all = valid.astype(jnp.float32)
    full = lax.all_to_all(
        lax.all_to_all(logits, "rows", split_axis=0, concat_axis=1, tiled=True),
        "vocab",
        split_axis=0,
        concat_axis=1,
        tiled=True,
    )
    z = full.astype(jnp.float32)
    my_eta = lax.dynamic_slice_in_dim(eta, first, share)
    my_teacher = lax.dynamic_slice_in_dim(teacher, first, share)
    my_live = lax.dynamic_slice_in_dim(live_all, first, share)
    columns = jnp.arange(z.shape[1], dtype=jnp.int32)
    peak = jnp.max(z, axis=1)
    e = jnp.exp(z - peak[:, None])
    total = jnp.sum(e, axis=1)
    spread = jnp.sum(e * (z - peak[:, None]), axis=1)
    kept, chosen, mass, target = cutoff_terms(z, e, total, spread, columns, my_eta, my_teacher)
    owned_grads, row_loss = finish(kept, chosen, mass, peak, target, my_live)
    grads = lax.all_to_all(
        lax.all_to_all(owned_grads, "vocab", split_axis=1, concat_axis=0, tiled=True),
        "rows",
        split_axis=1,
        concat_axis=0,
        tiled=True,
    )
    head_grad = lax.dot_general(
        grads, whole, (((0,), (0,)), ((), ())), preferred_element_type=jnp.float32
    )
    return (head_grad.astype(jnp.bfloat16), row_loss)


def solution(mesh):
    placed = (P("rows", None), P(None, ("vocab", "rows")), P(), P(), P())
    return jax.shard_map(
        per_device,
        mesh=mesh,
        in_specs=placed,
        out_specs=(P(("vocab", "rows"), None), P(("rows", "vocab"))),
        check_vma=False,
    )
```

profile of v0, /device:TPU:1, one launch (start us, length us, event | category | flops | bytes accessed | tf_op | source)
XLA Modules:
  0.0 156.0 jit_solution(7558896742063796071)
XLA Ops:
  7.2 0.0 all-gather.2.cloned.1.call-start
  7.2 0.7 all-gather.2.cloned.1.call-update
  7.9 16.8 %all-to-all-start = ((bf16[32,32,256]{2,1,0:T(8,128)(2,1)}), bf16[32,32,256]{2,1,0:T(8,128)(2,1)S(1)}, u32[]{:S(2)}, u32[]{:S(2)}) async-start(bf16[32,32,256]{2,1,0:T(8,128)(2,1)} %bitcast.21), calls=%async_computation | async-start | bytes 1048576 | tf_op jit(solution)/shard_map/all_to_all | solution.py:32
  24.7 0.7 convert_element_type.25
  25.4 0.8 dynamic_slice.11
  26.1 34.9 %all-to-all-done = bf16[32,32,256]{2,1,0:T(8,128)(2,1)S(1)} async-done(((bf16[32,32,256]{2,1,0:T(8,128)(2,1)}), bf16[32,32,256]{2,1,0:T(8,128)(2,1)S(1)}, u32[]{:S(2)}, u32[]{:S(2)}) %all-to-all-start) | async-done | bytes 524320 | tf_op jit(solution)/shard_map/all_to_all | solution.py:32
  61.0 0.3 copy.9
  61.3 0.9 all_to_all.49
  62.2 6.9 %all-to-all-start.1 = ((bf16[16,2,8192]{2,1,0:T(2,128)(2,1)}), bf16[16,2,8192]{2,1,0:T(2,128)(2,1)S(1)}, u32[]{:S(2)}, u32[]{:S(2)}) async-start(bf16[16,2,8192]{2,1,0:T(2,128)(2,1)} %all_to_all.49), calls=%async_computation.1 | async-start | bytes 1048576 | tf_op jit(solution)/shard_map/all_to_all | solution.py:31
  69.2 9.8 %all-to-all-done.1 = bf16[16,2,8192]{2,1,0:T(2,128)(2,1)S(1)} async-done(((bf16[16,2,8192]{2,1,0:T(2,128)(2,1)}), bf16[16,2,8192]{2,1,0:T(2,128)(2,1)S(1)}, u32[]{:S(2)}, u32[]{:S(2)}) %all-to-all-start.1) | async-done | bytes 524320 | tf_op jit(solution)/shard_map/all_to_all | solution.py:31
  79.0 1.2 reduce_max.14
  80.2 2.9 %fusion.1 = (f32[2]{0:T(128)S(1)}, f32[2]{0:T(128)S(1)}, f32[2]{0:T(128)S(1)}) fusion(bf16[16,2,8192]{2,1,0:T(2,128)(2,1)S(1)} %all-to-all-done.1, f32[2]{0:T(128)S(1)} %reduce_max.15, s32[2]{0:T(128)S(1)} %dynamic_slice.11, s32[16,8192]{1,0:T(8,128)S(1)} %multiply_add_fusion), kind=kLoop, calls=%fused_computation.8 | loop fusion | flops 2097146 | bytes 1048616 | tf_op jit(solution)/shard_map/reduce_sum | solution.py:46
  83.1 0.8 minimum_multiply_fusion
  83.9 1.8 %fusion.5 = (f32[2]{0:T(128)S(1)}, f32[2,16,8192]{2,0,1:T(2,128)S(1)}) fusion(s32[2]{0:T(128)S(1)} %dynamic_slice.11, s32[16,8192]{1,0:T(8,128)S(1)} %multiply_add_fusion, f32[2]{0:T(128)S(1)} %minimum_multiply_fusion, f32[2]{0:T(128)S(1)} %reduce_max.15, bf16[16,2,8192]{2,1,0:T(2,128)(2,1)S(1)} %all-to-all-done.1), kind=kLoop, calls=%fused_computation.16 | loop fusion | flops 1835006 | bytes 2097184 | tf_op jit(solution)/shard_map/reduce_sum | solution.py:13
  85.6 0.6 subtract_multiply_fusion
  86.2 0.9 fusion.4
  87.1 12.7 %all_to_all.61 = bf16[2,16,8192]{2,0,1:T(2,128)(2,1)S(1)} all-to-all(bf16[2,16,8192]{2,0,1:T(2,128)(2,1)S(1)} %fusion.4), channel_id=1, replica_groups=mesh['rows'=32,'vocab'=16] {'vocab'}, dimensions={1} | all-to-all | bytes 1048576 | tf_op jit(solution)/shard_map/all_to_all | solution.py:50
  99.8 0.3 all_to_all.53
  100.2 0.3 copy.10
  100.5 40.1 %all_to_all.62 = bf16[32,32,256]{2,0,1:T(8,128)(2,1)S(1)} all-to-all(bf16[32,32,256]{2,0,1:T(8,128)(2,1)S(1)} %copy.10), channel_id=1, replica_groups=mesh['rows'=32,'vocab'=16] {'rows'}, dimensions={1} | all-to-all | bytes 1048576 | tf_op jit(solution)/shard_map/all_to_all | solution.py:49
  140.6 0.0 all-gather.2.cloned.1.call-done
  140.6 8.6 %convolution_convert_fusion = bf16[256,5376]{1,0:T(8,128)(2,1)} fusion(bf16[1024,256]{1,0:T(8,128)(2,1)S(1)} %bitcast.18, bf16[1024,5376]{1,0:T(8,128)(2,1)} %all-gather.2.cloned.1.call-done), kind=kOutput, calls=%fused_computation | convolution fusion | flops 2819948544 | bytes 14286848 | tf_op jit(solution)/shard_map/dot_general | solution.py:56
  (2 shorter events, 0.0 us)
Async XLA Ops:
  7.2 133.4 %all-gather.2.cloned.1.call-start = ((), (), s32[]{:S(2)}) async-start(), calls=%async_computation.4 | async-start | bytes 11354112 | tf_op jit(solution)/shard_map/all_gather | solution.py:28
  7.9 53.1 %all-to-all-start = ((bf16[32,32,256]{2,1,0:T(8,128)(2,1)}), bf16[32,32,256]{2,1,0:T(8,128)(2,1)S(1)}, u32[]{:S(2)}, u32[]{:S(2)}) async-start(bf16[32,32,256]{2,1,0:T(8,128)(2,1)} %bitcast.21), calls=%async_computation | async-start | bytes 1048576 | tf_op jit(solution)/shard_map/all_to_all | solution.py:32
  62.2 16.8 %all-to-all-start.1 = ((bf16[16,2,8192]{2,1,0:T(2,128)(2,1)}), bf16[16,2,8192]{2,1,0:T(2,128)(2,1)S(1)}, u32[]{:S(2)}, u32[]{:S(2)}) async-start(bf16[16,2,8192]{2,1,0:T(2,128)(2,1)} %all_to_all.49), calls=%async_computation.1 | async-start | bytes 1048576 | tf_op jit(solution)/shard_map/all_to_all | solution.py:31
Sparse Core Ops, SparseCore 0:
  10.1 112.0 all-gather.1
where the time goes:
time: 157 us; the launch traced here: 156 us
  blocking collectives  52.8 us (34%)
  waiting for transfers between devices  45.4 us (29%)
  starting transfers between devices  23.7 us (15%)
  between operations  14.1 us (9%)
  other arithmetic  8.83 us (6%)
  matrix products  8.59 us (5%)
  local copies, waits for them, and re-layouts  2.59 us (2%)
    all_to_all x1, blocking collectives, per_device(): lax.all_to_all(lax.all_to_all(owned_grads, 'vocab', split_axis=1, concat_...  40.1 us
    all_to_all x1, waiting for transfers between devices, per_device(): lax.all_to_all(logits, 'rows', split_axis=0, concat_axis=1, tiled=True)  34.9 us
    all_to_all x1, starting transfers between devices, per_device(): lax.all_to_all(logits, 'rows', split_axis=0, concat_axis=1, tiled=True)  16.8 us
    all_to_all x1, blocking collectives, per_device(): lax.all_to_all(owned_grads, 'vocab', split_axis=1, concat_axis=0, tiled=T...  12.7 us
    all_to_all x1, waiting for transfers between devices, per_device(): lax.all_to_all(lax.all_to_all(logits, 'rows', split_axis=0, concat_axis=1...  9.84 us
    dot_general x1, matrix products, per_device(): lax.dot_general(grads, whole, (((0,), (0,)), ((), ())), preferred_element...  8.59 us
    all_to_all x1, starting transfers between devices, per_device(): lax.all_to_all(lax.all_to_all(logits, 'rows', split_axis=0, concat_axis=1...  6.88 us
  transfers between devices with their start and end apart: 3, of which 2 were waited for; matrix products, arithmetic and copies ran while one was open for 7% of the time, Pallas kernels for 0%

commit v1 on v0

v1 whole, which is shorter than its diff:
```python
import functools

import jax
import jax.numpy as jnp
from jax import lax
from jax.experimental import pallas as pl
from jax.experimental.pallas import tpu as pltpu
from jax.sharding import PartitionSpec as P

LANES = 128
F32 = jnp.float32


def local_stats(copies, logits_ref, rel_ref, zt_ref, out_ref, stat):
    groups = logits_ref.shape[0] // LANES
    for i in range(groups):
        z = logits_ref[i * LANES : (i + 1) * LANES, :].astype(F32).T
        zt_ref[:, i * LANES : (i + 1) * LANES] = z.astype(jnp.bfloat16)
        peak = jnp.max(z, axis=0, keepdims=True)
        below = z - peak
        e = jnp.exp(below)
        chosen = lax.broadcasted_iota(jnp.int32, z.shape, 0) == rel_ref[i : i + 1, :]
        stat[i : i + 1, :] = peak
        stat[groups + i : groups + i + 1, :] = jnp.sum(e, axis=0, keepdims=True)
        stat[2 * groups + i : 2 * groups + i + 1, :] = jnp.sum(e * below, axis=0, keepdims=True)
        stat[3 * groups + i : 3 * groups + i + 1, :] = jnp.sum(
            jnp.where(chosen, z, 0.0), axis=0, keepdims=True
        )
    for j in range(copies):
        out_ref[j] = stat[...]


def merged(parts_ref):
    n, depth, _ = parts_ref.shape
    g = depth // 4
    peak = parts_ref[0, :g, :]
    for j in range(1, n):
        peak = jnp.maximum(peak, parts_ref[j, :g, :])
    total = jnp.zeros_like(peak)
    spread = jnp.zeros_like(peak)
    target = jnp.zeros_like(peak)
    for j in range(n):
        gap = parts_ref[j, :g, :] - peak
        scale = jnp.exp(gap)
        part = parts_ref[j, g : 2 * g, :]
        total += scale * part
        spread += scale * (parts_ref[j, 2 * g : 3 * g, :] + gap * part)
        target += parts_ref[j, 3 * g :, :]
    return peak, total, spread, target


def merge_stats(copies, parts_ref, out_ref):
    peak, total, spread, target = merged(parts_ref)
    g = peak.shape[0]
    for j in range(copies):
        out_ref[j, :g, :] = peak
        out_ref[j, g : 2 * g, :] = total
        out_ref[j, 2 * g : 3 * g, :] = spread
        out_ref[j, 3 * g :, :] = target


def kept_of(zt_ref, i, peak, limit, rel):
    z = zt_ref[:, i * LANES : (i + 1) * LANES].astype(F32)
    e = jnp.exp(z - peak)
    chosen = lax.broadcasted_iota(jnp.int32, z.shape, 0) == rel
    return jnp.where((e > limit) | chosen, e, 0.0), chosen


def local_mass(copies, parts_ref, zt_ref, eta_ref, rel_ref, row_ref, out_ref, mass):
    peak, total, spread, target = merged(parts_ref)
    g = peak.shape[0]
    eta = eta_ref[...]
    entropy = jnp.log(total) - spread / total
    cutoff = jnp.minimum(eta, jnp.sqrt(eta) * jnp.exp(-entropy))
    row_ref[0] = peak
    row_ref[1] = cutoff * total
    row_ref[2] = target
    for i in range(g):
        at = slice(i, i + 1)
        kept, _ = kept_of(zt_ref, i, row_ref[0, at, :], row_ref[1, at, :], rel_ref[at, :])
        mass[at, :] = jnp.sum(kept, axis=0, keepdims=True)
    for j in range(copies):
        out_ref[j] = mass[...]


def merge_mass(copies, parts_ref, out_ref):
    mass = parts_ref[0]
    for j in range(1, parts_ref.shape[0]):
        mass += parts_ref[j]
    for j in range(copies):
        out_ref[j] = mass


def head_grad_kernel(
    parts_ref, row_ref, zt_ref, rel_ref, valid_ref, own_ref, hidden_ref, out_ref, loss_ref, mass, grads
):
    @pl.when(pl.program_id(0) == 0)
    def _():
        total = parts_ref[0]
        for j in range(1, parts_ref.shape[0]):
            total += parts_ref[j]
        mass[...] = total
        g = total.shape[0]
        live = valid_ref[...].astype(F32)
        loss = live * (jnp.log(total) + row_ref[0] - row_ref[2])
        place = lax.broadcasted_iota(jnp.int32, loss.shape, 0) * LANES + lax.broadcasted_iota(
            jnp.int32, loss.shape, 1
        )
        for k in range(loss_ref.shape[0]):
            loss_ref[k] = jnp.sum(jnp.where(place == own_ref[0] + k, loss, 0.0))
        for i in range(g):
            at = slice(i, i + 1)
            kept, chosen = kept_of(zt_ref, i, row_ref[0, at, :], row_ref[1, at, :], rel_ref[at, :])
            grads[:, i * LANES : (i + 1) * LANES] = (
                live[at, :] * (kept / mass[at, :] - chosen.astype(F32))
            ).astype(jnp.bfloat16)

    out_ref[...] = jnp.dot(grads[...], hidden_ref[...], preferred_element_type=F32).astype(
        out_ref.dtype
    )


VMEM = pl.BlockSpec(memory_space=pltpu.VMEM)
SMEM = pl.BlockSpec(memory_space=pltpu.SMEM)


def call(kernel, outs, scratch, flops, *args):
    moved = sum(a.size * a.dtype.itemsize for a in args) + sum(
        o.size * o.dtype.itemsize for o in jax.tree.leaves(outs)
    )
    return pl.pallas_call(
        kernel,
        out_shape=outs,
        in_specs=[VMEM] * len(args),
        out_specs=jax.tree.map(lambda _: VMEM, outs),
        scratch_shapes=scratch,
        compiler_params=pltpu.CompilerParams(vmem_limit_bytes=24 << 20),
        cost_estimate=pl.CostEstimate(flops=flops, bytes_accessed=moved, transcendentals=0),
    )(*args)


def spread_out(parts, axis):
    return lax.all_to_all(parts, axis, split_axis=0, concat_axis=0, tiled=True)


def per_device(hidden, logits, eta, teacher, valid):
    n_rows, n_vocab = lax.axis_size("rows"), lax.axis_size("vocab")
    rows, wide = logits.shape
    width = hidden.shape[1]
    g = rows // LANES
    whole = lax.all_gather(hidden, "rows", axis=0, tiled=True)
    at_rows, at_vocab = lax.axis_index("rows"), lax.axis_index("vocab")
    rel = (teacher - (at_vocab * n_rows + at_rows) * wide).reshape(g, LANES)
    share = rows // (n_rows * n_vocab)
    own = ((at_rows * n_vocab + at_vocab) * share).reshape(1)
    shape = jax.ShapeDtypeStruct

    zt, parts = call(
        functools.partial(local_stats, n_vocab),
        (shape((wide, rows), jnp.bfloat16), shape((n_vocab, 4 * g, LANES), F32)),
        [pltpu.VMEM((4 * g, LANES), F32)],
        20 * rows * wide,
        logits,
        rel,
    )
    parts = spread_out(parts, "vocab")
    parts = call(
        functools.partial(merge_stats, n_rows), shape((n_rows, 4 * g, LANES), F32), [], rows * 128, parts
    )
    parts = spread_out(parts, "rows")
    row_stats, masses = call(
        functools.partial(local_mass, n_vocab),
        (shape((3, g, LANES), F32), shape((n_vocab, g, LANES), F32)),
        [pltpu.VMEM((g, LANES), F32)],
        20 * rows * wide,
        parts,
        zt,
        eta.reshape(g, LANES),
        rel,
    )
    masses = spread_out(masses, "vocab")
    masses = call(
        functools.partial(merge_mass, n_rows), shape((n_rows, g, LANES), F32), [], rows * 16, masses
    )
    masses = spread_out(masses, "rows")

    tile = 768
    head_grad, row_loss = pl.pallas_call(
        head_grad_kernel,
        grid=(width // tile,),
        in_specs=[VMEM] * 5 + [SMEM, pl.BlockSpec((rows, tile), lambda j: (0, j))],
        out_specs=(pl.BlockSpec((wide, tile), lambda j: (0, j)), SMEM),
        out_shape=(shape((wide, width), jnp.bfloat16), shape((share,), F32)),
        scratch_shapes=[pltpu.VMEM((g, LANES), F32), pltpu.VMEM((wide, rows), jnp.bfloat16)],
        compiler_params=pltpu.CompilerParams(vmem_limit_bytes=56 << 20),
        cost_estimate=pl.CostEstimate(
            flops=2 * rows * wide * width,
            bytes_accessed=2 * (rows * width + wide * width),
            transcendentals=0,
        ),
    )(masses, row_stats, zt, rel, valid.reshape(g, LANES), own, whole)
    return head_grad, row_loss


def solution(mesh):
    placed = (P("rows", None), P(None, ("vocab", "rows")), P(), P(), P())
    return jax.shard_map(
        per_device,
        mesh=mesh,
        in_specs=placed,
        out_specs=(P(("vocab", "rows"), None), P(("rows", "vocab"))),
        check_vma=False,
    )
```

time: 157 us -> 144 us (0.917)
  blocking collectives: 52.8 us -> 80.9 us
  starting transfers between devices: 23.7 us -> 5.56 us
  waiting for transfers between devices: 45.4 us -> 28.3 us
  Pallas kernels: 0 us -> 11.9 us
  matrix products: 8.59 us -> 0 us
  other arithmetic: 8.83 us -> 0.69 us
    all_to_all x2 -> x3, blocking collectives: 52.8 us -> 80.9 us  [spread_out(): return lax.all_to_all(parts, axis, split_axis=0, concat_axis=0, tiled=True)]
    all_to_all x2 -> x1, waiting for transfers between devices: 44.8 us -> 18.2 us  [spread_out(): return lax.all_to_all(parts, axis, split_axis=0, concat_axis=0, tiled=True)]
    all_to_all x2 -> x1, starting transfers between devices: 23.6 us -> 5.52 us  [spread_out(): return lax.all_to_all(parts, axis, split_axis=0, concat_axis=0, tiled=True)]
    pallas_call x0 -> x5, Pallas kernels: none -> 11.9 us  [the longest x1 10.2 us: per_device(): pl.pallas_call(head_grad_kernel, grid=(width // tile,), in_specs=[VMEM] *...]
    all_gather x1, waiting for transfers between devices: 0.01 us -> 9.42 us  [per_device(): whole = lax.all_gather(hidden, 'rows', axis=0, tiled=True)]
    dot_general x1 -> x0, matrix products: 8.59 us -> none  [per_device(): lax.dot_general(grads, whole, (((0,), (0,)), ((), ())), preferred_element...]
    reduce_sum x2 -> x0, other arithmetic: 4.64 us -> none  [the longest x1 2.87 us: per_device(): spread = jnp.sum(e * (z - peak[:, None]), axis=1)]
    all_to_all x4 -> x0, local copies, waits for them, and re-layouts: 1.83 us -> none  [the longest x1 0.92 us: per_device(): lax.all_to_all(lax.all_to_all(logits, 'rows', split_axis=0, concat_axis=1...]
  transfers between devices with their start and end apart: 3 -> 2, of which waited for: 2 -> 2; matrix products, arithmetic and copies ran while one was open for 7% -> 0% of each run, Pallas kernels for 0% -> 1%
where the time goes in v1:
time: 144 us; the launch traced here: 143 us
  blocking collectives  80.9 us (56%)
  waiting for transfers between devices  28.3 us (20%)
  between operations  14.1 us (10%)
  Pallas kernels  11.9 us (8%)
  starting transfers between devices  5.56 us (4%)
  local copies, waits for them, and re-layouts  1.74 us (1%)
    all_to_all x3, blocking collectives, spread_out(): return lax.all_to_all(parts, axis, split_axis=0, concat_axis=0, tiled=True)  80.9 us
    all_to_all x1, waiting for transfers between devices, spread_out(): return lax.all_to_all(parts, axis, split_axis=0, concat_axis=0, tiled=True)  18.2 us
    pallas_call x1, Pallas kernels, per_device(): pl.pallas_call(head_grad_kernel, grid=(width // tile,), in_specs=[VMEM] *...  10.2 us
    all_gather x1, waiting for transfers between devices, per_device(): whole = lax.all_gather(hidden, 'rows', axis=0, tiled=True)  9.42 us
    all_to_all x1, starting transfers between devices, spread_out(): return lax.all_to_all(parts, axis, split_axis=0, concat_axis=0, tiled=True)  5.52 us
  transfers between devices with their start and end apart: 2, of which 2 were waited for; matrix products, arithmetic and copies ran while one was open for 0% of the time, Pallas kernels for 1%

profile of v1, /device:TPU:1, one launch (start us, length us, event | category | flops | bytes accessed | tf_op | source)
XLA Modules:
  0.0 143.3 jit_solution(16332626973838476189)
XLA Ops:
  7.2 0.0 all-gather.2.cloned.1.call-start
  7.2 0.7 all-gather.2.cloned.1.call-update
  7.9 0.7 subtract_bitcast_fusion.rel_ref
  8.6 0.0 copy-start.1
  8.6 1.0 copy-done.1
  9.6 0.0 copy-start.2
  9.6 0.6 shard_map.68
  10.2 0.0 copy-start
  10.2 14.8 %all_to_all.20.parts_ref = f32[16,32,128]{2,1,0:T(8,128)S(1)} all-to-all(f32[16,32,128]{2,1,0:T(8,128)S(1)} %get-tuple-element.6), channel_id=1, replica_groups=mesh['rows'=32,'vocab'=16] {'vocab'}, dimensions={0} | all-to-all | bytes 524288 | tf_op jit(solution)/shard_map/all_to_all | solution.py:143
  25.0 0.1 shard_map.69
  25.1 56.6 %all_to_all.21.parts_ref = f32[32,32,128]{2,1,0:T(8,128)S(1)} all-to-all(f32[32,32,128]{2,1,0:T(8,128)S(1)} %shard_map.69), channel_id=1, replica_groups=mesh['rows'=32,'vocab'=16] {'rows'}, dimensions={0} | all-to-all | bytes 1048576 | tf_op jit(solution)/shard_map/all_to_all | solution.py:143
  81.7 0.0 copy-start.4
  81.7 0.7 copy-done.4
  82.4 0.4 shard_map.70
  82.8 0.0 copy-start.3
  82.8 9.6 %all_to_all.22.parts_ref = f32[16,8,128]{2,1,0:T(8,128)S(1)} all-to-all(f32[16,8,128]{2,1,0:T(8,128)S(1)} %get-tuple-element.8), channel_id=1, replica_groups=mesh['rows'=32,'vocab'=16] {'vocab'}, dimensions={0} | all-to-all | bytes 131072 | tf_op jit(solution)/shard_map/all_to_all | solution.py:143
  92.4 0.0 copy-done.3
  92.4 0.7 shard_map.71
  93.1 5.5 %all-to-all-start.3 = ((f32[32,8,128]{2,1,0:T(8,128)}), f32[32,8,128]{2,1,0:T(8,128)S(1)}, u32[]{:S(2)}, u32[]{:S(2)}) async-start(f32[32,8,128]{2,1,0:T(8,128)} %shard_map.71), calls=%async_computation.3 | async-start | bytes 262144 | tf_op jit(solution)/shard_map/all_to_all | solution.py:143
  98.6 18.2 %all-to-all-done.3.parts_ref = f32[32,8,128]{2,1,0:T(8,128)S(1)} async-done(((f32[32,8,128]{2,1,0:T(8,128)}), f32[32,8,128]{2,1,0:T(8,128)S(1)}, u32[]{:S(2)}, u32[]{:S(2)}) %all-to-all-start.3) | async-done | bytes 131104 | tf_op jit(solution)/shard_map/all_to_all | solution.py:143
  116.8 0.0 copy-start.5
  116.8 9.4 %all-gather.2.cloned.1.call-done.hidden_ref = bf16[1024,5376]{1,0:T(8,128)(2,1)} async-done(((bf16[32,5376]{1,0:T(8,128)(2,1)}), bf16[1024,5376]{1,0:T(8,128)(2,1)}) %all-gather.2.cloned.1.call-update) | async-done | bytes 11010064 | tf_op jit(solution)/shard_map/all_gather | solution.py:151
  126.2 0.0 copy-done.2
  126.2 0.0 copy-done
  126.3 0.0 copy-done.5
  126.3 10.2 %shard_map.72 = (bf16[256,5376]{1,0:T(8,128)(2,1)}, f32[2]{0:T(128)}) custom-call(f32[32,8,128]{2,1,0:T(8,128)} %copy-done.5, f32[3,8,128]{2,1,0:T(8,128)} %copy-done.3, bf16[256,1024]{1,0:T(8,128)(2,1)} %copy-done, s32[8,128]{1,0:T(8,128)} %copy-done.2, s32[8,128]{1,0:T(8,128)} %bitcast.6, s32[1]{0:T(128)} %bitcast.3.own_ref, ...), custom_call_target="tpu_custom_call" | custom-call | flops 2818572288 | bytes 13762560 | tf_op jit(solution)/shard_map/pallas_call | solution.py:188
Async XLA Ops:
  7.2 119.1 %all-gather.2.cloned.1.call-start = ((), (), s32[]{:S(2)}) async-start(), calls=%async_computation.4 | async-start | bytes 11354112 | tf_op jit(solution)/shard_map/all_gather | solution.py:151
  8.6 1.0 copy-start.1
  9.6 116.6 %copy-start.2 = (s32[8,128]{1,0:T(8,128)}, s32[8,128]{1,0:T(8,128)S(1)}, u32[]{:S(2)}) copy-start(s32[8,128]{1,0:T(8,128)S(1)} %subtract_bitcast_fusion.rel_ref) | copy-start | bytes 12292
  10.2 116.0 %copy-start = (bf16[256,1024]{1,0:T(8,128)(2,1)}, bf16[256,1024]{1,0:T(8,128)(2,1)S(1)}, u32[]{:S(2)}) copy-start(bf16[256,1024]{1,0:T(8,128)(2,1)S(1)} %get-tuple-element.7.zt_ref) | copy-start | bytes 1572868
  81.7 0.7 copy-start.4
  82.8 9.6 %copy-start.3 = (f32[3,8,128]{2,1,0:T(8,128)}, f32[3,8,128]{2,1,0:T(8,128)S(1)}, u32[]{:S(2)}) copy-start(f32[3,8,128]{2,1,0:T(8,128)S(1)} %get-tuple-element.9.row_ref) | copy-start | bytes 36868
  93.1 23.8 %all-to-all-start.3 = ((f32[32,8,128]{2,1,0:T(8,128)}), f32[32,8,128]{2,1,0:T(8,128)S(1)}, u32[]{:S(2)}, u32[]{:S(2)}) async-start(f32[32,8,128]{2,1,0:T(8,128)} %shard_map.71), calls=%async_computation.3 | async-start | bytes 262144 | tf_op jit(solution)/shard_map/all_to_all | solution.py:143
  116.8 9.4 %copy-start.5 = (f32[32,8,128]{2,1,0:T(8,128)}, f32[32,8,128]{2,1,0:T(8,128)S(1)}, u32[]{:S(2)}) copy-start(f32[32,8,128]{2,1,0:T(8,128)S(1)} %all-to-all-done.3.parts_ref) | copy-start | bytes 393220
Sparse Core Ops, SparseCore 0:
  10.1 116.0 all-gather.1

commit v2 on v0

v2 whole, which is shorter than its diff:
```python
import functools

import jax
import jax.numpy as jnp
from jax import lax
from jax.experimental import pallas as pl
from jax.experimental.pallas import tpu as pltpu
from jax.sharding import Mesh
from jax.sharding import PartitionSpec as P

LANES = 128
F32 = jnp.float32
PEAK, TOTAL, SPREAD, TARGET, MASS = range(5)


def turned(columns):
    n = columns[0].shape[0]
    lane = lax.broadcasted_iota(jnp.int32, (n, LANES), 1)
    x = jnp.zeros((n, LANES), F32)
    for k, c in enumerate(columns):
        x = jnp.where(lane == k, c, x)
    x = jnp.concatenate([x, jnp.zeros((LANES - n, LANES), F32)], axis=0)
    return x.T[:8, :]


def chosen_at(teacher, source, z_at, n_z, shape):
    width = shape[1]
    base = ((source // 2 * n_z + z_at) * 2 + source % 2) * width
    return lax.broadcasted_iota(jnp.int32, shape, 1) + base == teacher


def share_stats(n_z, at_ref, logits_ref, teacher_ref, out_ref):
    n, rows, wide = logits_ref.shape
    half = wide // LANES
    teacher = teacher_ref[...]

    def block(s):
        return logits_ref[s].astype(F32)

    top = block(0)
    for s in range(1, n):
        top = jnp.maximum(top, block(s))
    peak = jnp.max(top, axis=1, keepdims=True)
    total = jnp.zeros((rows, wide), F32)
    spread = jnp.zeros((rows, wide), F32)
    target = jnp.zeros((rows, wide), F32)
    for s in range(n):
        z = block(s)
        below = z - peak
        e = jnp.exp(below)
        total += e
        spread += e * below
        target += jnp.where(chosen_at(teacher, s, at_ref[0], n_z, z.shape), z, 0.0)
    tile = turned([peak] + [jnp.sum(x, axis=1, keepdims=True) for x in (total, spread, target)])
    for j in range(out_ref.shape[0]):
        out_ref[j] = tile


def share_mass(n_z, at_ref, parts_ref, logits_ref, teacher_ref, eta_ref, row_ref, out_ref):
    n, rows, wide = logits_ref.shape
    parts = [parts_ref[j] for j in range(parts_ref.shape[0])]
    peak = parts[0][PEAK : PEAK + 1]
    for p in parts[1:]:
        peak = jnp.maximum(peak, p[PEAK : PEAK + 1])
    total = jnp.zeros_like(peak)
    spread = jnp.zeros_like(peak)
    target = jnp.zeros_like(peak)
    for p in parts:
        gap = p[PEAK : PEAK + 1] - peak
        scale = jnp.exp(gap)
        total += scale * p[TOTAL : TOTAL + 1]
        spread += scale * (p[SPREAD : SPREAD + 1] + gap * p[TOTAL : TOTAL + 1])
        target += p[TARGET : TARGET + 1]
    lane = lax.broadcasted_iota(jnp.int32, total.shape, 1)
    total = jnp.where(lane < rows, total, 1.0)
    eta = eta_ref[...]
    entropy = jnp.log(total) - spread / total
    cutoff = jnp.minimum(eta, jnp.sqrt(eta) * jnp.exp(-entropy))
    limit = cutoff * total
    tile = jnp.concatenate([peak, limit, target, jnp.zeros((5, LANES), F32)], axis=0)
    row_ref[...] = tile
    columns = jnp.concatenate([tile, jnp.zeros((LANES - 8, LANES), F32)], axis=0).T
    peak_c, limit_c = columns[:rows, 0:1], columns[:rows, 1:2]
    teacher = teacher_ref[...]
    mass = jnp.zeros((rows, wide), F32)
    for s in range(n):
        e = jnp.exp(logits_ref[s].astype(F32) - peak_c)
        chosen = chosen_at(teacher, s, at_ref[0], n_z, e.shape)
        mass += jnp.where((e > limit_c) | chosen, e, 0.0)
    tile = turned([jnp.sum(mass, axis=1, keepdims=True)])
    for j in range(out_ref.shape[0]):
        out_ref[j] = tile


def finish_rows(rows, at_ref, masses_ref, row_ref, out_ref):
    mass = masses_ref[0][:1]
    for j in range(1, masses_ref.shape[0]):
        mass += masses_ref[j][:1]
    row = row_ref[...]
    tile = jnp.concatenate([row[:3], mass, row[4:]], axis=0)
    lane = lax.broadcasted_iota(jnp.int32, tile.shape, 1)
    tile = jnp.where(lane < rows, tile, 0.0)
    per = LANES // rows
    placed = jnp.zeros_like(tile)
    for k in range(per):
        moved = pltpu.roll(tile, k * rows, 1) if k else tile
        placed = jnp.where(at_ref[0] % per == k, moved, placed)
    for j in range(out_ref.shape[0]):
        out_ref[j] = placed


def turn_logits(logits_ref, zt_ref):
    for i in range(logits_ref.shape[0] // LANES):
        at = slice(i * LANES, (i + 1) * LANES)
        zt_ref[:, at] = logits_ref[at, :].astype(F32).T.astype(jnp.bfloat16)


def logit_grads(own_ref, rows_ref, zt_ref, rel_ref, valid_ref, grads_ref, loss_ref):
    groups = zt_ref.shape[1] // LANES
    per = rows_ref.shape[0] // groups
    loss = [jnp.float32(0.0) for _ in range(loss_ref.shape[0])]
    for i in range(groups):
        tile = rows_ref[per * i]
        for k in range(1, per):
            tile += rows_ref[per * i + k]
        peak, limit, target, mass = (tile[k : k + 1] for k in range(4))
        live = valid_ref[i : i + 1, :].astype(F32)
        row_loss = live * (jnp.log(mass) + peak - target)
        place = lax.broadcasted_iota(jnp.int32, row_loss.shape, 1) + i * LANES
        for k in range(len(loss)):
            loss[k] += jnp.sum(jnp.where(place == own_ref[0] + k, row_loss, 0.0))
        at = slice(i * LANES, (i + 1) * LANES)
        z = zt_ref[:, at].astype(F32)
        e = jnp.exp(z - peak)
        chosen = lax.broadcasted_iota(jnp.int32, z.shape, 0) == rel_ref[i : i + 1, :]
        kept = jnp.where((e > limit) | chosen, e, 0.0)
        grads_ref[:, at] = (live * (kept / mass - chosen.astype(F32))).astype(jnp.bfloat16)
    for k in range(len(loss)):
        loss_ref[k] = loss[k]


def head_product(grads_ref, hidden_ref, out_ref):
    out_ref[...] = jnp.dot(grads_ref[...], hidden_ref[...], preferred_element_type=F32).astype(
        out_ref.dtype
    )


VMEM = pl.BlockSpec(memory_space=pltpu.VMEM)
SMEM = pl.BlockSpec(memory_space=pltpu.SMEM)


def call(kernel, outs, flops, *args, in_specs=None, out_specs=None):
    moved = sum(a.size * a.dtype.itemsize for a in args) + sum(
        o.size * o.dtype.itemsize for o in jax.tree.leaves(outs)
    )
    return pl.pallas_call(
        kernel,
        out_shape=outs,
        in_specs=in_specs or [SMEM if a.shape == (1,) else VMEM for a in args],
        out_specs=out_specs or jax.tree.map(lambda _: VMEM, outs),
        compiler_params=pltpu.CompilerParams(vmem_limit_bytes=24 << 20),
        cost_estimate=pl.CostEstimate(flops=flops, bytes_accessed=moved, transcendentals=0),
    )(*args)


def swap(parts, axis):
    return lax.all_to_all(parts, axis, split_axis=0, concat_axis=0, tiled=True)


def per_device(hidden, logits, eta, teacher, valid):
    n_z, n_vocab = lax.axis_size("z"), lax.axis_size("vocab")
    plane = ("vocab", "core")
    n_plane = 2 * n_vocab
    rows, wide = logits.shape
    width = hidden.shape[1]
    g = rows // LANES
    mine = rows // n_plane
    share = rows // (n_z * n_plane)
    shape = jax.ShapeDtypeStruct
    at_z, at_core, at_vocab = (lax.axis_index(a) for a in ("z", "core", "vocab"))
    at_plane = at_vocab * 2 + at_core

    whole = lax.all_gather(hidden, ("z", "core"), axis=0, tiled=True)

    mine_logits = swap(logits.reshape(n_plane, mine, wide), plane)
    zt = call(turn_logits, shape((wide, rows), jnp.bfloat16), rows * wide, logits)
    my_teacher = lax.dynamic_slice_in_dim(teacher, at_plane * mine, mine).reshape(mine, 1)
    my_eta = lax.dynamic_slice_in_dim(eta, at_plane * mine, mine)
    my_eta = jnp.pad(my_eta, (0, LANES - mine), constant_values=0.001).reshape(1, LANES)
    z_one = at_z.reshape(1)
    tiles = shape((n_z, 8, LANES), F32)
    parts = call(
        functools.partial(share_stats, n_z), tiles, 20 * rows * wide, z_one, mine_logits, my_teacher
    )
    row_stats, masses = call(
        functools.partial(share_mass, n_z),
        (shape((8, LANES), F32), tiles),
        20 * rows * wide,
        z_one,
        swap(parts, "z"),
        mine_logits,
        my_teacher,
        my_eta,
    )
    done = call(
        functools.partial(finish_rows, mine),
        shape((n_plane, 8, LANES), F32),
        rows * 16,
        at_plane.reshape(1),
        swap(masses, "z"),
        row_stats,
    )
    done = swap(done, plane)
    rel = (teacher - ((at_vocab * n_z + at_z) * 2 + at_core) * wide).reshape(g, LANES)
    own = (((at_z * 2 + at_core) * n_vocab + at_vocab) * share).reshape(1)
    grads, row_loss = call(
        logit_grads,
        (shape((wide, rows), jnp.bfloat16), shape((share,), F32)),
        20 * rows * wide,
        own,
        done,
        zt,
        rel,
        valid.reshape(g, LANES),
        out_specs=(VMEM, SMEM),
    )

    tile = 768
    head_grad = pl.pallas_call(
        head_product,
        grid=(width // tile,),
        in_specs=[VMEM, pl.BlockSpec((rows, tile), lambda j: (0, j))],
        out_specs=pl.BlockSpec((wide, tile), lambda j: (0, j)),
        out_shape=shape((wide, width), jnp.bfloat16),
        compiler_params=pltpu.CompilerParams(vmem_limit_bytes=56 << 20),
        cost_estimate=pl.CostEstimate(
            flops=2 * rows * wide * width,
            bytes_accessed=2 * (rows * width + wide * width),
            transcendentals=0,
        ),
    )(grads, whole)
    return head_grad, row_loss


def solution(mesh):
    n_rows, n_vocab = mesh.devices.shape
    split = Mesh(mesh.devices.reshape(n_rows // 2, 2, n_vocab), ("z", "core", "vocab"))
    rows, entries = ("z", "core"), ("vocab", "z", "core")
    return jax.shard_map(
        per_device,
        mesh=split,
        in_specs=(P(rows, None), P(None, entries), P(), P(), P()),
        out_specs=(P(entries, None), P(("z", "core", "vocab"))),
        check_vma=False,
    )
```

time: 157 us -> 121 us (0.77)
  blocking collectives: 52.8 us -> 0 us
  Pallas kernels: 0 us -> 13.9 us
  starting transfers between devices: 23.7 us -> 34 us
  matrix products: 8.59 us -> 0 us
  waiting for transfers between devices: 45.4 us -> 53.8 us
  other arithmetic: 8.83 us -> 0.69 us
    all_to_all x2 -> x0, blocking collectives: 52.8 us -> none  [the longest x1 40.1 us: per_device(): lax.all_to_all(lax.all_to_all(owned_grads, 'vocab', split_axis=1, concat_...]
    pallas_call x0 -> x6, Pallas kernels: none -> 13.9 us  [the longest x1 9.39 us: per_device(): pl.pallas_call(head_product, grid=(width // tile,), in_specs=[VMEM, pl.Bl...]
    all_gather x1, waiting for transfers between devices: 0.01 us -> 13.7 us  [per_device(): whole = lax.all_gather(hidden, ('z', 'core'), axis=0, tiled=True)]
    all_to_all x2 -> x4, starting transfers between devices: 23.6 us -> 34 us  [swap(): return lax.all_to_all(parts, axis, split_axis=0, concat_axis=0, tiled=True)]
    dot_general x1 -> x0, matrix products: 8.59 us -> none  [per_device(): lax.dot_general(grads, whole, (((0,), (0,)), ((), ())), preferred_element...]
    all_to_all x2 -> x4, waiting for transfers between devices: 44.8 us -> 39.5 us  [swap(): return lax.all_to_all(parts, axis, split_axis=0, concat_axis=0, tiled=True)]
    reduce_sum x2 -> x0, other arithmetic: 4.64 us -> none  [the longest x1 2.87 us: per_device(): spread = jnp.sum(e * (z - peak[:, None]), axis=1)]
    unnamed x0 -> x6, local copies, waits for them, and re-layouts: none -> 2.52 us
  transfers between devices with their start and end apart: 3 -> 5, of which waited for: 2 -> 5; matrix products, arithmetic and copies ran while one was open for 7% -> 2% of each run, Pallas kernels for 0% -> 4%
where the time goes in v2:
time: 121 us
  waiting for transfers between devices  53.8 us (44%)
  starting transfers between devices  34 us (28%)
  between operations  14.1 us (12%)
  Pallas kernels  13.9 us (11%)
  local copies, waits for them, and re-layouts  4.15 us (3%)
    all_to_all x4, waiting for transfers between devices, swap(): return lax.all_to_all(parts, axis, split_axis=0, concat_axis=0, tiled=True)  39.5 us
    all_to_all x4, starting transfers between devices, swap(): return lax.all_to_all(parts, axis, split_axis=0, concat_axis=0, tiled=True)  34 us
    all_gather x1, waiting for transfers between devices, per_device(): whole = lax.all_gather(hidden, ('z', 'core'), axis=0, tiled=True)  13.7 us
    pallas_call x1, Pallas kernels, per_device(): pl.pallas_call(head_product, grid=(width // tile,), in_specs=[VMEM, pl.Bl...  9.39 us
    pallas_call x5, Pallas kernels, call(): pl.pallas_call(kernel, out_shape=outs, in_specs=in_specs or [SMEM if a.sh...  4.54 us
    unnamed x6, local copies, waits for them, and re-layouts  2.52 us
  transfers between devices with their start and end apart: 5, of which 5 were waited for; matrix products, arithmetic and copies ran while one was open for 2% of the time, Pallas kernels for 4%

profile of v2, /device:TPU:1, one launch (start us, length us, event | category | flops | bytes accessed | tf_op | source)
XLA Modules:
  0.0 120.8 jit_solution(16750824279538008490)
XLA Ops:
  7.2 0.0 all-gather.2.cloned.1.call-start
  7.2 0.7 all-gather.2.cloned.1.call-update
  7.9 10.4 %all-to-all-start = ((bf16[32,32,256]{2,1,0:T(8,128)(2,1)}), bf16[32,32,256]{2,1,0:T(8,128)(2,1)S(1)}, u32[]{:S(2)}, u32[]{:S(2)}) async-start(bf16[32,32,256]{2,1,0:T(8,128)(2,1)} %bitcast.11), calls=%async_computation | async-start | bytes 1048576 | tf_op jit(solution)/shard_map/all_to_all | solution.py:167
  18.4 0.8 dynamic-slice_bitcast_fusion
  19.1 0.1 copy.7.teacher_ref
  19.2 10.9 %all-to-all-done.logits_ref = bf16[32,32,256]{2,1,0:T(8,128)(2,1)S(1)} async-done(((bf16[32,32,256]{2,1,0:T(8,128)(2,1)}), bf16[32,32,256]{2,1,0:T(8,128)(2,1)S(1)}, u32[]{:S(2)}, u32[]{:S(2)}) %all-to-all-start) | async-done | bytes 524320 | tf_op jit(solution)/shard_map/all_to_all | solution.py:167
  30.1 1.2 shard_map.68
  31.3 13.0 %all-to-all-start.1 = ((f32[16,8,128]{2,1,0:T(8,128)}), f32[16,8,128]{2,1,0:T(8,128)S(1)}, u32[]{:S(2)}, u32[]{:S(2)}) async-start(f32[16,8,128]{2,1,0:T(8,128)} %shard_map.68), calls=%async_computation.1 | async-start | bytes 131072 | tf_op jit(solution)/shard_map/all_to_all | solution.py:167
  44.2 0.8 dynamic_slice.7
  45.0 11.0 %all-to-all-done.1.parts_ref = f32[16,8,128]{2,1,0:T(8,128)S(1)} async-done(((f32[16,8,128]{2,1,0:T(8,128)}), f32[16,8,128]{2,1,0:T(8,128)S(1)}, u32[]{:S(2)}, u32[]{:S(2)}) %all-to-all-start.1) | async-done | bytes 65568 | tf_op jit(solution)/shard_map/all_to_all | solution.py:167
  56.1 1.2 %shard_map.69 = (f32[8,128]{1,0:T(8,128)S(1)}, f32[16,8,128]{2,1,0:T(8,128)}) custom-call(s32[1]{0:T(128)} %bitcast.2.at_ref, f32[16,8,128]{2,1,0:T(8,128)S(1)} %all-to-all-done.1.parts_ref, bf16[32,32,256]{2,1,0:T(8,128)(2,1)S(1)} %all-to-all-done.logits_ref, s32[32,1]{1,0:T(8,128)S(1)} %copy.7.teacher_ref, f32[1,128]{1,0:T(1,128)S(1)} %pad_bitcast_fusion.eta_ref), custom_call_target="tpu_custom_call" | custom-call | flops 5242880 | bytes 660100 | tf_op jit(solution)/shard_map/pallas_call | solution.py:156
  57.3 4.7 %all-to-all-start.2 = ((f32[16,8,128]{2,1,0:T(8,128)}), f32[16,8,128]{2,1,0:T(8,128)S(1)}, u32[]{:S(2)}, u32[]{:S(2)}) async-start(f32[16,8,128]{2,1,0:T(8,128)} %get-tuple-element.6), calls=%async_computation.2 | async-start | bytes 131072 | tf_op jit(solution)/shard_map/all_to_all | solution.py:167
  62.0 0.0 copy-start
  62.0 1.0 copy-done
  63.0 0.2 shard_map.71.zt_ref
  63.3 10.6 %all-to-all-done.2.masses_ref = f32[16,8,128]{2,1,0:T(8,128)S(1)} async-done(((f32[16,8,128]{2,1,0:T(8,128)}), f32[16,8,128]{2,1,0:T(8,128)S(1)}, u32[]{:S(2)}, u32[]{:S(2)}) %all-to-all-start.2) | async-done | bytes 65568 | tf_op jit(solution)/shard_map/all_to_all | solution.py:167
  73.8 0.8 shard_map.70
  74.6 5.9 %all-to-all-start.3 = ((f32[32,8,128]{2,1,0:T(8,128)}), f32[32,8,128]{2,1,0:T(8,128)S(1)}, u32[]{:S(2)}, u32[]{:S(2)}) async-start(f32[32,8,128]{2,1,0:T(8,128)} %shard_map.70), calls=%async_computation.3 | async-start | bytes 262144 | tf_op jit(solution)/shard_map/all_to_all | solution.py:167
  80.5 0.7 subtract_bitcast_fusion.rel_ref
  81.2 7.0 %all-to-all-done.3.rows_ref = f32[32,8,128]{2,1,0:T(8,128)S(1)} async-done(((f32[32,8,128]{2,1,0:T(8,128)}), f32[32,8,128]{2,1,0:T(8,128)S(1)}, u32[]{:S(2)}, u32[]{:S(2)}) %all-to-all-start.3) | async-done | bytes 131104 | tf_op jit(solution)/shard_map/all_to_all | solution.py:167
  88.2 0.0 copy-start.2
  88.2 0.7 copy-done.2
  88.9 1.1 shard_map.72
  90.1 0.0 copy-start.1
  90.1 0.8 copy-done.1
  90.9 13.7 %all-gather.2.cloned.1.call-done.hidden_ref = bf16[1024,5376]{1,0:T(8,128)(2,1)} async-done(((bf16[32,5376]{1,0:T(8,128)(2,1)}), bf16[1024,5376]{1,0:T(8,128)(2,1)}) %all-gather.2.cloned.1.call-update) | async-done | bytes 11010064 | tf_op jit(solution)/shard_map/all_gather | solution.py:183
  104.5 9.4 %shard_map.73 = bf16[256,5376]{1,0:T(8,128)(2,1)} custom-call(bf16[256,1024]{1,0:T(8,128)(2,1)} %copy-done.1, bf16[1024,5376]{1,0:T(8,128)(2,1)} %all-gather.2.cloned.1.call-done.hidden_ref), custom_call_target="tpu_custom_call" | custom-call | flops 2818572288 | bytes 13762560 | tf_op jit(solution)/shard_map/pallas_call | solution.py:229
  (1 shorter events, 0.0 us)
Async XLA Ops:
  7.2 97.4 %all-gather.2.cloned.1.call-start = ((), (), s32[]{:S(2)}) async-start(), calls=%async_computation.4 | async-start | bytes 11354112 | tf_op jit(solution)/shard_map/all_gather | solution.py:183
  7.9 22.2 %all-to-all-start = ((bf16[32,32,256]{2,1,0:T(8,128)(2,1)}), bf16[32,32,256]{2,1,0:T(8,128)(2,1)S(1)}, u32[]{:S(2)}, u32[]{:S(2)}) async-start(bf16[32,32,256]{2,1,0:T(8,128)(2,1)} %bitcast.11), calls=%async_computation | async-start | bytes 1048576 | tf_op jit(solution)/shard_map/all_to_all | solution.py:167
  31.3 24.8 %all-to-all-start.1 = ((f32[16,8,128]{2,1,0:T(8,128)}), f32[16,8,128]{2,1,0:T(8,128)S(1)}, u32[]{:S(2)}, u32[]{:S(2)}) async-start(f32[16,8,128]{2,1,0:T(8,128)} %shard_map.68), calls=%async_computation.1 | async-start | bytes 131072 | tf_op jit(solution)/shard_map/all_to_all | solution.py:167
  57.3 16.5 %all-to-all-start.2 = ((f32[16,8,128]{2,1,0:T(8,128)}), f32[16,8,128]{2,1,0:T(8,128)S(1)}, u32[]{:S(2)}, u32[]{:S(2)}) async-start(f32[16,8,128]{2,1,0:T(8,128)} %get-tuple-element.6), calls=%async_computation.2 | async-start | bytes 131072 | tf_op jit(solution)/shard_map/all_to_all | solution.py:167
  62.0 1.0 copy-start
  74.6 13.6 %all-to-all-start.3 = ((f32[32,8,128]{2,1,0:T(8,128)}), f32[32,8,128]{2,1,0:T(8,128)S(1)}, u32[]{:S(2)}, u32[]{:S(2)}) async-start(f32[32,8,128]{2,1,0:T(8,128)} %shard_map.70), calls=%async_computation.3 | async-start | bytes 262144 | tf_op jit(solution)/shard_map/all_to_all | solution.py:167
  88.2 0.7 copy-start.2
  90.1 0.8 copy-start.1
Sparse Core Ops, SparseCore 0:
  10.1 94.3 all-gather.1

commit v3 on v2

--- a/solution.py
+++ b/solution.py
@@ -10,7 +10,6 @@
 
 LANES = 128
 F32 = jnp.float32
-PEAK, TOTAL, SPREAD, TARGET, MASS = range(5)
 
 
 def turned(columns):
@@ -20,7 +19,13 @@
     for k, c in enumerate(columns):
         x = jnp.where(lane == k, c, x)
     x = jnp.concatenate([x, jnp.zeros((LANES - n, LANES), F32)], axis=0)
-    return x.T[:8, :]
+    x = x.T[:8, :]
+    lane = lax.broadcasted_iota(jnp.int32, (1, LANES), 1)
+    row = jnp.zeros((1, LANES), F32)
+    for k in range(len(columns)):
+        moved = pltpu.roll(x[k : k + 1], k * n, 1) if k else x[:1]
+        row = jnp.where(lane // n == k, moved, row)
+    return row
 
 
 def chosen_at(teacher, source, z_at, n_z, shape):
@@ -58,19 +63,16 @@
 
 def share_mass(n_z, at_ref, parts_ref, logits_ref, teacher_ref, eta_ref, row_ref, out_ref):
     n, rows, wide = logits_ref.shape
-    parts = [parts_ref[j] for j in range(parts_ref.shape[0])]
-    peak = parts[0][PEAK : PEAK + 1]
-    for p in parts[1:]:
-        peak = jnp.maximum(peak, p[PEAK : PEAK + 1])
-    total = jnp.zeros_like(peak)
-    spread = jnp.zeros_like(peak)
-    target = jnp.zeros_like(peak)
-    for p in parts:
-        gap = p[PEAK : PEAK + 1] - peak
-        scale = jnp.exp(gap)
-        total += scale * p[TOTAL : TOTAL + 1]
-        spread += scale * (p[SPREAD : SPREAD + 1] + gap * p[TOTAL : TOTAL + 1])
-        target += p[TARGET : TARGET + 1]
+    parts = jnp.concatenate([parts_ref[j] for j in range(parts_ref.shape[0])], axis=0)
+    tops, totals, spreads, targets = (
+        pltpu.roll(parts, LANES - k * rows, 1) if k else parts for k in range(4)
+    )
+    peak = jnp.max(tops, axis=0, keepdims=True)
+    gap = tops - peak
+    scale = jnp.exp(jnp.minimum(gap, 0.0))
+    total = jnp.sum(scale * totals, axis=0, keepdims=True)
+    spread = jnp.sum(scale * (spreads + gap * totals), axis=0, keepdims=True)
+    target = jnp.sum(targets, axis=0, keepdims=True)
     lane = lax.broadcasted_iota(jnp.int32, total.shape, 1)
     total = jnp.where(lane < rows, total, 1.0)
     eta = eta_ref[...]
@@ -93,9 +95,9 @@
 
 
 def finish_rows(rows, at_ref, masses_ref, row_ref, out_ref):
-    mass = masses_ref[0][:1]
+    mass = masses_ref[0]
     for j in range(1, masses_ref.shape[0]):
-        mass += masses_ref[j][:1]
+        mass += masses_ref[j]
     row = row_ref[...]
     tile = jnp.concatenate([row[:3], mass, row[4:]], axis=0)
     lane = lax.broadcasted_iota(jnp.int32, tile.shape, 1)
@@ -139,10 +141,29 @@
         loss_ref[k] = loss[k]
 
 
-def head_product(grads_ref, hidden_ref, out_ref):
-    out_ref[...] = jnp.dot(grads_ref[...], hidden_ref[...], preferred_element_type=F32).astype(
-        out_ref.dtype
-    )
+def head_product(widths, ahead, grads_ref, hidden_ref, out_ref, held, result, in_sems, out_sems):
+    starts = [sum(widths[:i]) for i in range(len(widths))]
+    at = [pl.ds(s, w) for s, w in zip(starts, widths)]
+    into = [
+        pltpu.make_async_copy(hidden_ref.at[:, a], held.at[:, a], in_sems.at[i])
+        for i, a in enumerate(at)
+    ]
+    out = [
+        pltpu.make_async_copy(result.at[:, a], out_ref.at[:, a], out_sems.at[i])
+        for i, a in enumerate(at)
+    ]
+    for copy in into[:ahead]:
+        copy.start()
+    for i, (s, w) in enumerate(zip(starts, widths)):
+        into[i].wait()
+        if i + ahead < len(widths):
+            into[i + ahead].start()
+        result[:, s : s + w] = jnp.dot(
+            grads_ref[...], held[:, s : s + w], preferred_element_type=F32
+        ).astype(result.dtype)
+        out[i].start()
+    for copy in out:
+        copy.wait()
 
 
 VMEM = pl.BlockSpec(memory_space=pltpu.VMEM)
@@ -188,7 +209,7 @@
     my_eta = lax.dynamic_slice_in_dim(eta, at_plane * mine, mine)
     my_eta = jnp.pad(my_eta, (0, LANES - mine), constant_values=0.001).reshape(1, LANES)
     z_one = at_z.reshape(1)
-    tiles = shape((n_z, 8, LANES), F32)
+    tiles = shape((n_z, 1, LANES), F32)
     parts = call(
         functools.partial(share_stats, n_z), tiles, 20 * rows * wide, z_one, mine_logits, my_teacher
     )
@@ -225,13 +246,22 @@
         out_specs=(VMEM, SMEM),
     )
 
-    tile = 768
+    widths, left = [512], width - 512
+    while left:
+        widths.append(min(1024, left))
+        left -= widths[-1]
+    any_space = pl.BlockSpec(memory_space=pl.ANY)
     head_grad = pl.pallas_call(
-        head_product,
-        grid=(width // tile,),
-        in_specs=[VMEM, pl.BlockSpec((rows, tile), lambda j: (0, j))],
-        out_specs=pl.BlockSpec((wide, tile), lambda j: (0, j)),
+        functools.partial(head_product, widths, 3),
+        in_specs=[VMEM, any_space],
+        out_specs=any_space,
         out_shape=shape((wide, width), jnp.bfloat16),
+        scratch_shapes=[
+            pltpu.VMEM((rows, width), jnp.bfloat16),
+            pltpu.VMEM((wide, width), jnp.bfloat16),
+            pltpu.SemaphoreType.DMA((len(widths),)),
+            pltpu.SemaphoreType.DMA((len(widths),)),
+        ],
         compiler_params=pltpu.CompilerParams(vmem_limit_bytes=56 << 20),
         cost_estimate=pl.CostEstimate(
             flops=2 * rows * wide * width,

time: 121 us -> 114 us (0.942)
  waiting for transfers between devices: 53.8 us -> 49.5 us
  Pallas kernels: 13.9 us -> 12.1 us
    all_gather x1, waiting for transfers between devices: 13.7 us -> 10.5 us  [per_device(): whole = lax.all_gather(hidden, ('z', 'core'), axis=0, tiled=True)]
    pallas_call x1, Pallas kernels: 9.39 us -> 7.55 us  [per_device(): pl.pallas_call(functools.partial(head_product, widths, 3), in_specs=[VMEM...]
where the time goes in v3:
time: 114 us
  waiting for transfers between devices  49.5 us (43%)
  starting transfers between devices  33.2 us (29%)
  between operations  14.1 us (12%)
  Pallas kernels  12.1 us (11%)
  local copies, waits for them, and re-layouts  4.13 us (4%)
    all_to_all x4, waiting for transfers between devices, swap(): return lax.all_to_all(parts, axis, split_axis=0, concat_axis=0, tiled=True)  38.3 us
    all_to_all x4, starting transfers between devices, swap(): return lax.all_to_all(parts, axis, split_axis=0, concat_axis=0, tiled=True)  33.2 us
    all_gather x1, waiting for transfers between devices, per_device(): whole = lax.all_gather(hidden, ('z', 'core'), axis=0, tiled=True)  10.5 us
    pallas_call x1, Pallas kernels, per_device(): pl.pallas_call(functools.partial(head_product, widths, 3), in_specs=[VMEM...  7.55 us
    pallas_call x5, Pallas kernels, call(): pl.pallas_call(kernel, out_shape=outs, in_specs=in_specs or [SMEM if a.sh...  4.59 us
    unnamed x6, local copies, waits for them, and re-layouts  2.52 us
  transfers between devices with their start and end apart: 5, of which 5 were waited for; matrix products, arithmetic and copies ran while one was open for 2% of the time, Pallas kernels for 4%

profile of v3, /device:TPU:1, one launch (start us, length us, event | category | flops | bytes accessed | tf_op | source)
XLA Modules:
  0.0 113.8 jit_solution(4313234790942662644)
XLA Ops:
  7.2 0.0 all-gather.2.cloned.1.call-start
  7.2 0.7 all-gather.2.cloned.1.call-update
  7.9 10.4 %all-to-all-start = ((bf16[32,32,256]{2,1,0:T(8,128)(2,1)}), bf16[32,32,256]{2,1,0:T(8,128)(2,1)S(1)}, u32[]{:S(2)}, u32[]{:S(2)}) async-start(bf16[32,32,256]{2,1,0:T(8,128)(2,1)} %bitcast.11), calls=%async_computation | async-start | bytes 1048576 | tf_op jit(solution)/shard_map/all_to_all | solution.py:188
  18.3 0.8 dynamic_slice.7
  19.1 0.8 dynamic-slice_bitcast_fusion
  19.9 0.1 copy.7.teacher_ref
  20.0 10.1 %all-to-all-done.logits_ref = bf16[32,32,256]{2,1,0:T(8,128)(2,1)S(1)} async-done(((bf16[32,32,256]{2,1,0:T(8,128)(2,1)}), bf16[32,32,256]{2,1,0:T(8,128)(2,1)S(1)}, u32[]{:S(2)}, u32[]{:S(2)}) %all-to-all-start) | async-done | bytes 524320 | tf_op jit(solution)/shard_map/all_to_all | solution.py:188
  30.1 1.2 %shard_map.68 = f32[16,1,128]{2,1,0:T(1,128)} custom-call(s32[1]{0:T(128)} %bitcast.2.at_ref, bf16[32,32,256]{2,1,0:T(8,128)(2,1)S(1)} %all-to-all-done.logits_ref, s32[32,1]{1,0:T(8,128)S(1)} %copy.7.teacher_ref), custom_call_target="tpu_custom_call" | custom-call | flops 5242880 | bytes 532612 | tf_op jit(solution)/shard_map/pallas_call | solution.py:177
  31.3 13.0 %all-to-all-start.1 = ((f32[16,1,128]{2,1,0:T(1,128)}), f32[16,1,128]{2,1,0:T(1,128)S(1)}, u32[]{:S(2)}, u32[]{:S(2)}) async-start(f32[16,1,128]{2,1,0:T(1,128)} %shard_map.68), calls=%async_computation.1 | async-start | bytes 16384 | tf_op jit(solution)/shard_map/all_to_all | solution.py:188
  44.3 11.3 %all-to-all-done.1.parts_ref = f32[16,1,128]{2,1,0:T(1,128)S(1)} async-done(((f32[16,1,128]{2,1,0:T(1,128)}), f32[16,1,128]{2,1,0:T(1,128)S(1)}, u32[]{:S(2)}, u32[]{:S(2)}) %all-to-all-start.1) | async-done | bytes 8224 | tf_op jit(solution)/shard_map/all_to_all | solution.py:188
  55.6 1.3 %shard_map.69 = (f32[8,128]{1,0:T(8,128)S(1)}, f32[16,1,128]{2,1,0:T(1,128)}) custom-call(s32[1]{0:T(128)} %bitcast.2.at_ref, f32[16,1,128]{2,1,0:T(1,128)S(1)} %all-to-all-done.1.parts_ref, bf16[32,32,256]{2,1,0:T(8,128)(2,1)S(1)} %all-to-all-done.logits_ref, s32[32,1]{1,0:T(8,128)S(1)} %copy.7.teacher_ref, f32[1,128]{1,0:T(1,128)S(1)} %pad_bitcast_fusion.eta_ref), custom_call_target="tpu_custom_call" | custom-call | flops 5242880 | bytes 545412 | tf_op jit(solution)/shard_map/pallas_call | solution.py:177
  56.8 3.5 %all-to-all-start.2 = ((f32[16,1,128]{2,1,0:T(1,128)}), f32[16,1,128]{2,1,0:T(1,128)S(1)}, u32[]{:S(2)}, u32[]{:S(2)}) async-start(f32[16,1,128]{2,1,0:T(1,128)} %get-tuple-element.6), calls=%async_computation.2 | async-start | bytes 16384 | tf_op jit(solution)/shard_map/all_to_all | solution.py:188
  60.3 0.0 copy-start
  60.3 1.0 copy-done
  61.4 0.2 shard_map.71.zt_ref
  61.6 9.9 %all-to-all-done.2.masses_ref = f32[16,1,128]{2,1,0:T(1,128)S(1)} async-done(((f32[16,1,128]{2,1,0:T(1,128)}), f32[16,1,128]{2,1,0:T(1,128)S(1)}, u32[]{:S(2)}, u32[]{:S(2)}) %all-to-all-start.2) | async-done | bytes 8224 | tf_op jit(solution)/shard_map/all_to_all | solution.py:188
  71.5 0.8 shard_map.70
  72.2 6.3 %all-to-all-start.3 = ((f32[32,8,128]{2,1,0:T(8,128)}), f32[32,8,128]{2,1,0:T(8,128)S(1)}, u32[]{:S(2)}, u32[]{:S(2)}) async-start(f32[32,8,128]{2,1,0:T(8,128)} %shard_map.70), calls=%async_computation.3 | async-start | bytes 262144 | tf_op jit(solution)/shard_map/all_to_all | solution.py:188
  78.6 0.7 subtract_bitcast_fusion.rel_ref
  79.2 7.0 %all-to-all-done.3.rows_ref = f32[32,8,128]{2,1,0:T(8,128)S(1)} async-done(((f32[32,8,128]{2,1,0:T(8,128)}), f32[32,8,128]{2,1,0:T(8,128)S(1)}, u32[]{:S(2)}, u32[]{:S(2)}) %all-to-all-start.3) | async-done | bytes 131104 | tf_op jit(solution)/shard_map/all_to_all | solution.py:188
  86.3 0.0 copy-start.2
  86.3 0.7 copy-done.2
  86.9 1.1 %shard_map.72 = (bf16[256,1024]{1,0:T(8,128)(2,1)S(1)}, f32[2]{0:T(128)}) custom-call(s32[1]{0:T(128)} %bitcast.own_ref, f32[32,8,128]{2,1,0:T(8,128)S(1)} %all-to-all-done.3.rows_ref, bf16[256,1024]{1,0:T(8,128)(2,1)S(1)} %shard_map.71.zt_ref, s32[8,128]{1,0:T(8,128)S(1)} %subtract_bitcast_fusion.rel_ref, s32[8,128]{1,0:T(8,128)S(1)} %bitcast.12), custom_call_target="tpu_custom_call" | custom-call | flops 5242880 | bytes 1187852 | tf_op jit(solution)/shard_map/pallas_call | solution.py:177
  88.1 0.0 copy-start.1
  88.1 0.8 copy-done.1
  88.9 10.5 %all-gather.2.cloned.1.call-done.hidden_ref = bf16[1024,5376]{1,0:T(8,128)(2,1)} async-done(((bf16[32,5376]{1,0:T(8,128)(2,1)}), bf16[1024,5376]{1,0:T(8,128)(2,1)}) %all-gather.2.cloned.1.call-update) | async-done | bytes 11010064 | tf_op jit(solution)/shard_map/all_gather | solution.py:204
  99.4 7.5 %shard_map.73 = bf16[256,5376]{1,0:T(8,128)(2,1)} custom-call(bf16[256,1024]{1,0:T(8,128)(2,1)} %copy-done.1, bf16[1024,5376]{1,0:T(8,128)(2,1)} %all-gather.2.cloned.1.call-done.hidden_ref), custom_call_target="tpu_custom_call" | custom-call | flops 2818572288 | bytes 13762560 | tf_op jit(solution)/shard_map/pallas_call | solution.py:254
  (1 shorter events, 0.0 us)
Async XLA Ops:
  7.2 92.2 %all-gather.2.cloned.1.call-start = ((), (), s32[]{:S(2)}) async-start(), calls=%async_computation.4 | async-start | bytes 11354112 | tf_op jit(solution)/shard_map/all_gather | solution.py:204
  7.9 22.2 %all-to-all-start = ((bf16[32,32,256]{2,1,0:T(8,128)(2,1)}), bf16[32,32,256]{2,1,0:T(8,128)(2,1)S(1)}, u32[]{:S(2)}, u32[]{:S(2)}) async-start(bf16[32,32,256]{2,1,0:T(8,128)(2,1)} %bitcast.11), calls=%async_computation | async-start | bytes 1048576 | tf_op jit(solution)/shard_map/all_to_all | solution.py:188
  31.3 24.3 %all-to-all-start.1 = ((f32[16,1,128]{2,1,0:T(1,128)}), f32[16,1,128]{2,1,0:T(1,128)S(1)}, u32[]{:S(2)}, u32[]{:S(2)}) async-start(f32[16,1,128]{2,1,0:T(1,128)} %shard_map.68), calls=%async_computation.1 | async-start | bytes 16384 | tf_op jit(solution)/shard_map/all_to_all | solution.py:188
  56.8 14.7 %all-to-all-start.2 = ((f32[16,1,128]{2,1,0:T(1,128)}), f32[16,1,128]{2,1,0:T(1,128)S(1)}, u32[]{:S(2)}, u32[]{:S(2)}) async-start(f32[16,1,128]{2,1,0:T(1,128)} %get-tuple-element.6), calls=%async_computation.2 | async-start | bytes 16384 | tf_op jit(solution)/shard_map/all_to_all | solution.py:188
  60.3 1.0 copy-start
  72.2 14.0 %all-to-all-start.3 = ((f32[32,8,128]{2,1,0:T(8,128)}), f32[32,8,128]{2,1,0:T(8,128)S(1)}, u32[]{:S(2)}, u32[]{:S(2)}) async-start(f32[32,8,128]{2,1,0:T(8,128)} %shard_map.70), calls=%async_computation.3 | async-start | bytes 262144 | tf_op jit(solution)/shard_map/all_to_all | solution.py:188
  86.3 0.7 copy-start.2
  88.1 0.8 copy-start.1
Sparse Core Ops, SparseCore 0:
  10.1 89.2 all-gather.1

commit v4 on v3

--- a/solution.py
+++ b/solution.py
@@ -111,30 +111,46 @@
         out_ref[j] = placed
 
 
-def turn_logits(logits_ref, zt_ref):
-    for i in range(logits_ref.shape[0] // LANES):
-        at = slice(i * LANES, (i + 1) * LANES)
-        zt_ref[:, at] = logits_ref[at, :].astype(F32).T.astype(jnp.bfloat16)
-
-
-def logit_grads(own_ref, rows_ref, zt_ref, rel_ref, valid_ref, grads_ref, loss_ref):
+def owner_at(place, n_z):
+    return place % n_z * 2 + place // n_z
+
+
+def turn_logits(n_z, logits_ref, zt_ref):
+    rows = logits_ref.shape[0]
+    mine = rows // (2 * n_z)
+    per = LANES // mine
+    for i in range(rows // LANES):
+        owners = [owner_at(i * per + k, n_z) for k in range(per)]
+        block = jnp.concatenate([logits_ref[j * mine : (j + 1) * mine, :] for j in owners], axis=0)
+        zt_ref[:, i * LANES : (i + 1) * LANES] = block.astype(F32).T.astype(jnp.bfloat16)
+
+
+def logit_grads(n_z, at_ref, rows_ref, zt_ref, codes_ref, grads_ref, loss_ref):
     groups = zt_ref.shape[1] // LANES
-    per = rows_ref.shape[0] // groups
+    mine = zt_ref.shape[1] // (2 * n_z)
+    per = LANES // mine
     loss = [jnp.float32(0.0) for _ in range(loss_ref.shape[0])]
+    lane = lax.broadcasted_iota(jnp.int32, (1, LANES), 1)
     for i in range(groups):
-        tile = rows_ref[per * i]
-        for k in range(1, per):
-            tile += rows_ref[per * i + k]
+        tile = jnp.zeros(rows_ref.shape[1:], F32)
+        codes = jnp.zeros((1, LANES), jnp.int32)
+        for k in range(per):
+            j = owner_at(i * per + k, n_z)
+            tile += rows_ref[j]
+            code = codes_ref[j // per : j // per + 1, :]
+            shift = (k - j % per) * mine % LANES
+            code = pltpu.roll(code, shift, 1) if shift else code
+            codes = jnp.where(lane // mine == k, code, codes)
         peak, limit, target, mass = (tile[k : k + 1] for k in range(4))
-        live = valid_ref[i : i + 1, :].astype(F32)
+        live = (codes & 1).astype(F32)
+        rel = (codes >> 1) - at_ref[1]
         row_loss = live * (jnp.log(mass) + peak - target)
-        place = lax.broadcasted_iota(jnp.int32, row_loss.shape, 1) + i * LANES
         for k in range(len(loss)):
-            loss[k] += jnp.sum(jnp.where(place == own_ref[0] + k, row_loss, 0.0))
+            loss[k] += jnp.sum(jnp.where(lane + i * LANES == at_ref[0] + k, row_loss, 0.0))
         at = slice(i * LANES, (i + 1) * LANES)
         z = zt_ref[:, at].astype(F32)
         e = jnp.exp(z - peak)
-        chosen = lax.broadcasted_iota(jnp.int32, z.shape, 0) == rel_ref[i : i + 1, :]
+        chosen = lax.broadcasted_iota(jnp.int32, z.shape, 0) == rel
         kept = jnp.where((e > limit) | chosen, e, 0.0)
         grads_ref[:, at] = (live * (kept / mass - chosen.astype(F32))).astype(jnp.bfloat16)
     for k in range(len(loss)):
@@ -170,14 +186,14 @@
 SMEM = pl.BlockSpec(memory_space=pltpu.SMEM)
 
 
-def call(kernel, outs, flops, *args, in_specs=None, out_specs=None):
+def call(kernel, outs, flops, *args, out_specs=None):
     moved = sum(a.size * a.dtype.itemsize for a in args) + sum(
         o.size * o.dtype.itemsize for o in jax.tree.leaves(outs)
     )
     return pl.pallas_call(
         kernel,
         out_shape=outs,
-        in_specs=in_specs or [SMEM if a.shape == (1,) else VMEM for a in args],
+        in_specs=[SMEM if a.size < 8 else VMEM for a in args],
         out_specs=out_specs or jax.tree.map(lambda _: VMEM, outs),
         compiler_params=pltpu.CompilerParams(vmem_limit_bytes=24 << 20),
         cost_estimate=pl.CostEstimate(flops=flops, bytes_accessed=moved, transcendentals=0),
@@ -201,10 +217,10 @@
     at_z, at_core, at_vocab = (lax.axis_index(a) for a in ("z", "core", "vocab"))
     at_plane = at_vocab * 2 + at_core
 
-    whole = lax.all_gather(hidden, ("z", "core"), axis=0, tiled=True)
+    whole = lax.all_gather(hidden, ("core", "z"), axis=0, tiled=True)
 
     mine_logits = swap(logits.reshape(n_plane, mine, wide), plane)
-    zt = call(turn_logits, shape((wide, rows), jnp.bfloat16), rows * wide, logits)
+    zt = call(functools.partial(turn_logits, n_z), shape((wide, rows), jnp.bfloat16), rows * wide, logits)
     my_teacher = lax.dynamic_slice_in_dim(teacher, at_plane * mine, mine).reshape(mine, 1)
     my_eta = lax.dynamic_slice_in_dim(eta, at_plane * mine, mine)
     my_eta = jnp.pad(my_eta, (0, LANES - mine), constant_values=0.001).reshape(1, LANES)
@@ -227,22 +243,22 @@
         functools.partial(finish_rows, mine),
         shape((n_plane, 8, LANES), F32),
         rows * 16,
-        at_plane.reshape(1),
+        (at_plane % 2 * n_z + at_plane // 2).reshape(1),
         swap(masses, "z"),
         row_stats,
     )
     done = swap(done, plane)
-    rel = (teacher - ((at_vocab * n_z + at_z) * 2 + at_core) * wide).reshape(g, LANES)
-    own = (((at_z * 2 + at_core) * n_vocab + at_vocab) * share).reshape(1)
+    codes = (teacher * 2 + valid).reshape(g, LANES)
+    own = (at_core * n_z + at_z) * mine + at_vocab * share
+    base = ((at_vocab * n_z + at_z) * 2 + at_core) * wide
     grads, row_loss = call(
-        logit_grads,
+        functools.partial(logit_grads, n_z),
         (shape((wide, rows), jnp.bfloat16), shape((share,), F32)),
         20 * rows * wide,
-        own,
+        jnp.stack([own, base]),
         done,
         zt,
-        rel,
-        valid.reshape(g, LANES),
+        codes,
         out_specs=(VMEM, SMEM),
     )
 

time: 114 us -> 115 us (level)
    unnamed x6 -> x4, local copies, waits for them, and re-layouts: 2.52 us -> 1.85 us
  transfers between devices with their start and end apart: 5 -> 5, of which waited for: 5 -> 5; matrix products, arithmetic and copies ran while one was open for 2% -> 2% of each run, Pallas kernels for 4% -> 5%
where the time goes in v4:
time: 115 us; the launch traced here: 114 us
  waiting for transfers between devices  49.7 us (43%)
  starting transfers between devices  33.2 us (29%)
  between operations  14.2 us (12%)
  Pallas kernels  12.8 us (11%)
  local copies, waits for them, and re-layouts  3.47 us (3%)
    all_to_all x4, waiting for transfers between devices, swap(): return lax.all_to_all(parts, axis, split_axis=0, concat_axis=0, tiled=True)  38.3 us
    all_to_all x4, starting transfers between devices, swap(): return lax.all_to_all(parts, axis, split_axis=0, concat_axis=0, tiled=True)  33.2 us
    all_gather x1, waiting for transfers between devices, per_device(): whole = lax.all_gather(hidden, ('core', 'z'), axis=0, tiled=True)  10.7 us
    pallas_call x1, Pallas kernels, per_device(): pl.pallas_call(functools.partial(head_product, widths, 3), in_specs=[VMEM...  7.55 us
    pallas_call x5, Pallas kernels, call(): pl.pallas_call(kernel, out_shape=outs, in_specs=[SMEM if a.size < 8 else...  5.3 us
  transfers between devices with their start and end apart: 5, of which 5 were waited for; matrix products, arithmetic and copies ran while one was open for 2% of the time, Pallas kernels for 5%

profile of v4, /device:TPU:1, one launch (start us, length us, event | category | flops | bytes accessed | tf_op | source)
XLA Modules:
  0.0 114.1 jit_solution(8234349606872213517)
XLA Ops:
  7.2 0.0 all-gather.2.cloned.1.call-start
  7.2 0.7 all-gather.2.cloned.1.call-update
  7.9 10.4 %all-to-all-start = ((bf16[32,32,256]{2,1,0:T(8,128)(2,1)}), bf16[32,32,256]{2,1,0:T(8,128)(2,1)S(1)}, u32[]{:S(2)}, u32[]{:S(2)}) async-start(bf16[32,32,256]{2,1,0:T(8,128)(2,1)} %bitcast.11), calls=%async_computation | async-start | bytes 1048576 | tf_op jit(solution)/shard_map/all_to_all | solution.py:204
  18.3 0.8 dynamic_slice.7
  19.1 0.8 dynamic-slice_bitcast_fusion
  19.9 0.1 copy.7.teacher_ref
  20.0 10.1 %all-to-all-done.logits_ref = bf16[32,32,256]{2,1,0:T(8,128)(2,1)S(1)} async-done(((bf16[32,32,256]{2,1,0:T(8,128)(2,1)}), bf16[32,32,256]{2,1,0:T(8,128)(2,1)S(1)}, u32[]{:S(2)}, u32[]{:S(2)}) %all-to-all-start) | async-done | bytes 524320 | tf_op jit(solution)/shard_map/all_to_all | solution.py:204
  30.1 1.2 %shard_map.68 = f32[16,1,128]{2,1,0:T(1,128)} custom-call(s32[1]{0:T(128)} %bitcast.3.at_ref, bf16[32,32,256]{2,1,0:T(8,128)(2,1)S(1)} %all-to-all-done.logits_ref, s32[32,1]{1,0:T(8,128)S(1)} %copy.7.teacher_ref), custom_call_target="tpu_custom_call" | custom-call | flops 5242880 | bytes 532612 | tf_op jit(solution)/shard_map/pallas_call | solution.py:193
  31.3 13.0 %all-to-all-start.1 = ((f32[16,1,128]{2,1,0:T(1,128)}), f32[16,1,128]{2,1,0:T(1,128)S(1)}, u32[]{:S(2)}, u32[]{:S(2)}) async-start(f32[16,1,128]{2,1,0:T(1,128)} %shard_map.68), calls=%async_computation.1 | async-start | bytes 16384 | tf_op jit(solution)/shard_map/all_to_all | solution.py:204
  44.3 11.3 %all-to-all-done.1.parts_ref = f32[16,1,128]{2,1,0:T(1,128)S(1)} async-done(((f32[16,1,128]{2,1,0:T(1,128)}), f32[16,1,128]{2,1,0:T(1,128)S(1)}, u32[]{:S(2)}, u32[]{:S(2)}) %all-to-all-start.1) | async-done | bytes 8224 | tf_op jit(solution)/shard_map/all_to_all | solution.py:204
  55.6 1.3 %shard_map.69 = (f32[8,128]{1,0:T(8,128)S(1)}, f32[16,1,128]{2,1,0:T(1,128)}) custom-call(s32[1]{0:T(128)} %bitcast.3.at_ref, f32[16,1,128]{2,1,0:T(1,128)S(1)} %all-to-all-done.1.parts_ref, bf16[32,32,256]{2,1,0:T(8,128)(2,1)S(1)} %all-to-all-done.logits_ref, s32[32,1]{1,0:T(8,128)S(1)} %copy.7.teacher_ref, f32[1,128]{1,0:T(1,128)S(1)} %pad_bitcast_fusion.eta_ref), custom_call_target="tpu_custom_call" | custom-call | flops 5242880 | bytes 545412 | tf_op jit(solution)/shard_map/pallas_call | solution.py:193
  56.8 3.5 %all-to-all-start.2 = ((f32[16,1,128]{2,1,0:T(1,128)}), f32[16,1,128]{2,1,0:T(1,128)S(1)}, u32[]{:S(2)}, u32[]{:S(2)}) async-start(f32[16,1,128]{2,1,0:T(1,128)} %get-tuple-element.6), calls=%async_computation.2 | async-start | bytes 16384 | tf_op jit(solution)/shard_map/all_to_all | solution.py:204
  60.3 11.3 %all-to-all-done.2.masses_ref = f32[16,1,128]{2,1,0:T(1,128)S(1)} async-done(((f32[16,1,128]{2,1,0:T(1,128)}), f32[16,1,128]{2,1,0:T(1,128)S(1)}, u32[]{:S(2)}, u32[]{:S(2)}) %all-to-all-start.2) | async-done | bytes 8224 | tf_op jit(solution)/shard_map/all_to_all | solution.py:204
  71.6 0.8 shard_map.70
  72.4 6.3 %all-to-all-start.3 = ((f32[32,8,128]{2,1,0:T(8,128)}), f32[32,8,128]{2,1,0:T(8,128)S(1)}, u32[]{:S(2)}, u32[]{:S(2)}) async-start(f32[32,8,128]{2,1,0:T(8,128)} %shard_map.70), calls=%async_computation.3 | async-start | bytes 262144 | tf_op jit(solution)/shard_map/all_to_all | solution.py:204
  78.7 0.7 add_bitcast_fusion.codes_ref
  79.4 0.0 copy-start
  79.4 1.1 copy-done
  80.4 0.2 shard_map.71.zt_ref
  80.7 0.1 pad_add_fusion.at_ref
  80.7 5.6 %all-to-all-done.3.rows_ref = f32[32,8,128]{2,1,0:T(8,128)S(1)} async-done(((f32[32,8,128]{2,1,0:T(8,128)}), f32[32,8,128]{2,1,0:T(8,128)S(1)}, u32[]{:S(2)}, u32[]{:S(2)}) %all-to-all-start.3) | async-done | bytes 131104 | tf_op jit(solution)/shard_map/all_to_all | solution.py:204
  86.4 1.9 %shard_map.72 = (bf16[256,1024]{1,0:T(8,128)(2,1)S(1)}, f32[2]{0:T(128)}) custom-call(s32[2]{0:T(128)S(1)} %pad_add_fusion.at_ref, f32[32,8,128]{2,1,0:T(8,128)S(1)} %all-to-all-done.3.rows_ref, bf16[256,1024]{1,0:T(8,128)(2,1)S(1)} %shard_map.71.zt_ref, s32[8,128]{1,0:T(8,128)S(1)} %add_bitcast_fusion.codes_ref), custom_call_target="tpu_custom_call" | custom-call | flops 5242880 | bytes 1183760 | tf_op jit(solution)/shard_map/pallas_call | solution.py:193
  88.2 0.0 copy-start.1
  88.2 0.8 copy-done.1
  89.0 10.7 %all-gather.2.cloned.1.call-done.hidden_ref = bf16[1024,5376]{1,0:T(8,128)(2,1)} async-done(((bf16[32,5376]{1,0:T(8,128)(2,1)}), bf16[1024,5376]{1,0:T(8,128)(2,1)}) %all-gather.2.cloned.1.call-update) | async-done | bytes 11010064 | tf_op jit(solution)/shard_map/all_gather | solution.py:220
  99.7 7.5 %shard_map.73 = bf16[256,5376]{1,0:T(8,128)(2,1)} custom-call(bf16[256,1024]{1,0:T(8,128)(2,1)} %copy-done.1, bf16[1024,5376]{1,0:T(8,128)(2,1)} %all-gather.2.cloned.1.call-done.hidden_ref), custom_call_target="tpu_custom_call" | custom-call | flops 2818572288 | bytes 13762560 | tf_op jit(solution)/shard_map/pallas_call | solution.py:270
  (1 shorter events, 0.0 us)
Async XLA Ops:
  7.2 92.5 %all-gather.2.cloned.1.call-start = ((), (), s32[]{:S(2)}) async-start(), calls=%async_computation.4 | async-start | bytes 11354112 | tf_op jit(solution)/shard_map/all_gather | solution.py:220
  7.9 22.2 %all-to-all-start = ((bf16[32,32,256]{2,1,0:T(8,128)(2,1)}), bf16[32,32,256]{2,1,0:T(8,128)(2,1)S(1)}, u32[]{:S(2)}, u32[]{:S(2)}) async-start(bf16[32,32,256]{2,1,0:T(8,128)(2,1)} %bitcast.11), calls=%async_computation | async-start | bytes 1048576 | tf_op jit(solution)/shard_map/all_to_all | solution.py:204
  31.3 24.3 %all-to-all-start.1 = ((f32[16,1,128]{2,1,0:T(1,128)}), f32[16,1,128]{2,1,0:T(1,128)S(1)}, u32[]{:S(2)}, u32[]{:S(2)}) async-start(f32[16,1,128]{2,1,0:T(1,128)} %shard_map.68), calls=%async_computation.1 | async-start | bytes 16384 | tf_op jit(solution)/shard_map/all_to_all | solution.py:204
  56.8 14.8 %all-to-all-start.2 = ((f32[16,1,128]{2,1,0:T(1,128)}), f32[16,1,128]{2,1,0:T(1,128)S(1)}, u32[]{:S(2)}, u32[]{:S(2)}) async-start(f32[16,1,128]{2,1,0:T(1,128)} %get-tuple-element.6), calls=%async_computation.2 | async-start | bytes 16384 | tf_op jit(solution)/shard_map/all_to_all | solution.py:204
  72.4 14.0 %all-to-all-start.3 = ((f32[32,8,128]{2,1,0:T(8,128)}), f32[32,8,128]{2,1,0:T(8,128)S(1)}, u32[]{:S(2)}, u32[]{:S(2)}) async-start(f32[32,8,128]{2,1,0:T(8,128)} %shard_map.70), calls=%async_computation.3 | async-start | bytes 262144 | tf_op jit(solution)/shard_map/all_to_all | solution.py:204
  79.4 1.1 copy-start
  88.2 0.8 copy-start.1
Sparse Core Ops, SparseCore 0:
  10.1 89.5 all-gather.1

commit v5 on v4

--- a/solution.py
+++ b/solution.py
@@ -157,27 +157,31 @@
         loss_ref[k] = loss[k]
 
 
-def head_product(widths, ahead, grads_ref, hidden_ref, out_ref, held, result, in_sems, out_sems):
-    starts = [sum(widths[:i]) for i in range(len(widths))]
-    at = [pl.ds(s, w) for s, w in zip(starts, widths)]
-    into = [
-        pltpu.make_async_copy(hidden_ref.at[:, a], held.at[:, a], in_sems.at[i])
-        for i, a in enumerate(at)
-    ]
-    out = [
-        pltpu.make_async_copy(result.at[:, a], out_ref.at[:, a], out_sems.at[i])
-        for i, a in enumerate(at)
-    ]
-    for copy in into[:ahead]:
-        copy.start()
-    for i, (s, w) in enumerate(zip(starts, widths)):
-        into[i].wait()
-        if i + ahead < len(widths):
-            into[i + ahead].start()
-        result[:, s : s + w] = jnp.dot(
-            grads_ref[...], held[:, s : s + w], preferred_element_type=F32
-        ).astype(result.dtype)
-        out[i].start()
+def head_product(tile, grads_ref, hidden_ref, out_ref, weights, held, total, result, sems, out_sems):
+    rows, width = hidden_ref.shape
+    half = rows // 2
+    lower, upper = pl.ds(0, half), pl.ds(half, half)
+    first = pltpu.make_async_copy(hidden_ref.at[lower], held.at[lower], sems.at[0])
+    second = pltpu.make_async_copy(hidden_ref.at[upper], held.at[upper], sems.at[1])
+    left = pltpu.make_async_copy(grads_ref, weights, sems.at[2])
+    left.start()
+    first.start()
+    second.start()
+    starts = list(range(0, width, tile))
+    left.wait()
+    first.wait()
+    for s in starts:
+        at = slice(s, min(s + tile, width))
+        total[:, at] = jnp.dot(weights[:, :half], held[:half, at], preferred_element_type=F32)
+    second.wait()
+    out = []
+    for i, s in enumerate(starts):
+        at = slice(s, min(s + tile, width))
+        more = jnp.dot(weights[:, half:], held[half:, at], preferred_element_type=F32)
+        result[:, at] = (total[:, at] + more).astype(result.dtype)
+        part = pl.ds(s, min(tile, width - s))
+        out.append(pltpu.make_async_copy(result.at[:, part], out_ref.at[:, part], out_sems.at[i]))
+        out[-1].start()
     for copy in out:
         copy.wait()
 
@@ -262,21 +266,20 @@
         out_specs=(VMEM, SMEM),
     )
 
-    widths, left = [512], width - 512
-    while left:
-        widths.append(min(1024, left))
-        left -= widths[-1]
+    tile = 768
     any_space = pl.BlockSpec(memory_space=pl.ANY)
     head_grad = pl.pallas_call(
-        functools.partial(head_product, widths, 3),
-        in_specs=[VMEM, any_space],
+        functools.partial(head_product, tile),
+        in_specs=[any_space, any_space],
         out_specs=any_space,
         out_shape=shape((wide, width), jnp.bfloat16),
         scratch_shapes=[
+            pltpu.VMEM((wide, rows), jnp.bfloat16),
             pltpu.VMEM((rows, width), jnp.bfloat16),
+            pltpu.VMEM((wide, width), F32),
             pltpu.VMEM((wide, width), jnp.bfloat16),
-            pltpu.SemaphoreType.DMA((len(widths),)),
-            pltpu.SemaphoreType.DMA((len(widths),)),
+            pltpu.SemaphoreType.DMA((3,)),
+            pltpu.SemaphoreType.DMA((-(-width // tile),)),
         ],
         compiler_params=pltpu.CompilerParams(vmem_limit_bytes=56 << 20),
         cost_estimate=pl.CostEstimate(

time: 115 us -> 114 us (level)
  no operation moved by 1% of the time
where the time goes in v5:
time: 114 us; the launch traced here: 113 us
  waiting for transfers between devices  49.7 us (44%)
  starting transfers between devices  33.2 us (29%)
  between operations  14.2 us (12%)
  Pallas kernels  12.1 us (11%)
  local copies, waits for them, and re-layouts  3.47 us (3%)
    all_to_all x4, waiting for transfers between devices, swap(): return lax.all_to_all(parts, axis, split_axis=0, concat_axis=0, tiled=True)  38.3 us
    all_to_all x4, starting transfers between devices, swap(): return lax.all_to_all(parts, axis, split_axis=0, concat_axis=0, tiled=True)  33.2 us
    all_gather x1, waiting for transfers between devices, per_device(): whole = lax.all_gather(hidden, ('core', 'z'), axis=0, tiled=True)  10.7 us
    pallas_call x1, Pallas kernels, per_device(): pl.pallas_call(functools.partial(head_product, tile), in_specs=[any_space...  6.83 us
    pallas_call x5, Pallas kernels, call(): pl.pallas_call(kernel, out_shape=outs, in_specs=[SMEM if a.size < 8 else...  5.3 us
  transfers between devices with their start and end apart: 5, of which 5 were waited for; matrix products, arithmetic and copies ran while one was open for 2% of the time, Pallas kernels for 5%

profile of v5, /device:TPU:1, one launch (start us, length us, event | category | flops | bytes accessed | tf_op | source)
XLA Modules:
  0.0 113.4 jit_solution(10772469704487055793)
XLA Ops:
  7.2 0.0 all-gather.2.cloned.1.call-start
  7.2 0.7 all-gather.2.cloned.1.call-update
  7.9 10.4 %all-to-all-start = ((bf16[32,32,256]{2,1,0:T(8,128)(2,1)}), bf16[32,32,256]{2,1,0:T(8,128)(2,1)S(1)}, u32[]{:S(2)}, u32[]{:S(2)}) async-start(bf16[32,32,256]{2,1,0:T(8,128)(2,1)} %bitcast.11), calls=%async_computation | async-start | bytes 1048576 | tf_op jit(solution)/shard_map/all_to_all | solution.py:208
  18.3 0.8 dynamic_slice.7
  19.1 0.8 dynamic-slice_bitcast_fusion
  19.9 0.1 copy.7.teacher_ref
  20.0 10.1 %all-to-all-done.logits_ref = bf16[32,32,256]{2,1,0:T(8,128)(2,1)S(1)} async-done(((bf16[32,32,256]{2,1,0:T(8,128)(2,1)}), bf16[32,32,256]{2,1,0:T(8,128)(2,1)S(1)}, u32[]{:S(2)}, u32[]{:S(2)}) %all-to-all-start) | async-done | bytes 524320 | tf_op jit(solution)/shard_map/all_to_all | solution.py:208
  30.1 1.2 %shard_map.68 = f32[16,1,128]{2,1,0:T(1,128)} custom-call(s32[1]{0:T(128)} %bitcast.3.at_ref, bf16[32,32,256]{2,1,0:T(8,128)(2,1)S(1)} %all-to-all-done.logits_ref, s32[32,1]{1,0:T(8,128)S(1)} %copy.7.teacher_ref), custom_call_target="tpu_custom_call" | custom-call | flops 5242880 | bytes 532612 | tf_op jit(solution)/shard_map/pallas_call | solution.py:197
  31.3 13.0 %all-to-all-start.1 = ((f32[16,1,128]{2,1,0:T(1,128)}), f32[16,1,128]{2,1,0:T(1,128)S(1)}, u32[]{:S(2)}, u32[]{:S(2)}) async-start(f32[16,1,128]{2,1,0:T(1,128)} %shard_map.68), calls=%async_computation.1 | async-start | bytes 16384 | tf_op jit(solution)/shard_map/all_to_all | solution.py:208
  44.3 11.3 %all-to-all-done.1.parts_ref = f32[16,1,128]{2,1,0:T(1,128)S(1)} async-done(((f32[16,1,128]{2,1,0:T(1,128)}), f32[16,1,128]{2,1,0:T(1,128)S(1)}, u32[]{:S(2)}, u32[]{:S(2)}) %all-to-all-start.1) | async-done | bytes 8224 | tf_op jit(solution)/shard_map/all_to_all | solution.py:208
  55.6 1.3 %shard_map.69 = (f32[8,128]{1,0:T(8,128)S(1)}, f32[16,1,128]{2,1,0:T(1,128)}) custom-call(s32[1]{0:T(128)} %bitcast.3.at_ref, f32[16,1,128]{2,1,0:T(1,128)S(1)} %all-to-all-done.1.parts_ref, bf16[32,32,256]{2,1,0:T(8,128)(2,1)S(1)} %all-to-all-done.logits_ref, s32[32,1]{1,0:T(8,128)S(1)} %copy.7.teacher_ref, f32[1,128]{1,0:T(1,128)S(1)} %pad_bitcast_fusion.eta_ref), custom_call_target="tpu_custom_call" | custom-call | flops 5242880 | bytes 545412 | tf_op jit(solution)/shard_map/pallas_call | solution.py:197
  56.8 3.5 %all-to-all-start.2 = ((f32[16,1,128]{2,1,0:T(1,128)}), f32[16,1,128]{2,1,0:T(1,128)S(1)}, u32[]{:S(2)}, u32[]{:S(2)}) async-start(f32[16,1,128]{2,1,0:T(1,128)} %get-tuple-element.6), calls=%async_computation.2 | async-start | bytes 16384 | tf_op jit(solution)/shard_map/all_to_all | solution.py:208
  60.3 11.3 %all-to-all-done.2.masses_ref = f32[16,1,128]{2,1,0:T(1,128)S(1)} async-done(((f32[16,1,128]{2,1,0:T(1,128)}), f32[16,1,128]{2,1,0:T(1,128)S(1)}, u32[]{:S(2)}, u32[]{:S(2)}) %all-to-all-start.2) | async-done | bytes 8224 | tf_op jit(solution)/shard_map/all_to_all | solution.py:208
  71.6 0.8 shard_map.70
  72.4 6.3 %all-to-all-start.3 = ((f32[32,8,128]{2,1,0:T(8,128)}), f32[32,8,128]{2,1,0:T(8,128)S(1)}, u32[]{:S(2)}, u32[]{:S(2)}) async-start(f32[32,8,128]{2,1,0:T(8,128)} %shard_map.70), calls=%async_computation.3 | async-start | bytes 262144 | tf_op jit(solution)/shard_map/all_to_all | solution.py:208
  78.7 0.7 add_bitcast_fusion.codes_ref
  79.4 0.0 copy-start
  79.4 1.1 copy-done
  80.4 0.2 shard_map.71.zt_ref
  80.7 0.1 pad_add_fusion.at_ref
  80.7 5.6 %all-to-all-done.3.rows_ref = f32[32,8,128]{2,1,0:T(8,128)S(1)} async-done(((f32[32,8,128]{2,1,0:T(8,128)}), f32[32,8,128]{2,1,0:T(8,128)S(1)}, u32[]{:S(2)}, u32[]{:S(2)}) %all-to-all-start.3) | async-done | bytes 131104 | tf_op jit(solution)/shard_map/all_to_all | solution.py:208
  86.4 1.9 %shard_map.72 = (bf16[256,1024]{1,0:T(8,128)(2,1)S(1)}, f32[2]{0:T(128)}) custom-call(s32[2]{0:T(128)S(1)} %pad_add_fusion.at_ref, f32[32,8,128]{2,1,0:T(8,128)S(1)} %all-to-all-done.3.rows_ref, bf16[256,1024]{1,0:T(8,128)(2,1)S(1)} %shard_map.71.zt_ref, s32[8,128]{1,0:T(8,128)S(1)} %add_bitcast_fusion.codes_ref), custom_call_target="tpu_custom_call" | custom-call | flops 5242880 | bytes 1183760 | tf_op jit(solution)/shard_map/pallas_call | solution.py:197
  88.2 0.0 copy-start.1
  88.2 0.8 copy-done.1
  89.0 10.7 %all-gather.2.cloned.1.call-done.hidden_ref = bf16[1024,5376]{1,0:T(8,128)(2,1)} async-done(((bf16[32,5376]{1,0:T(8,128)(2,1)}), bf16[1024,5376]{1,0:T(8,128)(2,1)}) %all-gather.2.cloned.1.call-update) | async-done | bytes 11010064 | tf_op jit(solution)/shard_map/all_gather | solution.py:224
  99.7 6.8 %shard_map.73 = bf16[256,5376]{1,0:T(8,128)(2,1)} custom-call(bf16[256,1024]{1,0:T(8,128)(2,1)} %copy-done.1, bf16[1024,5376]{1,0:T(8,128)(2,1)} %all-gather.2.cloned.1.call-done.hidden_ref), custom_call_target="tpu_custom_call" | custom-call | flops 2818572288 | bytes 13762560 | tf_op jit(solution)/shard_map/pallas_call | solution.py:271
  (1 shorter events, 0.0 us)
Async XLA Ops:
  7.2 92.5 %all-gather.2.cloned.1.call-start = ((), (), s32[]{:S(2)}) async-start(), calls=%async_computation.4 | async-start | bytes 11354112 | tf_op jit(solution)/shard_map/all_gather | solution.py:224
  7.9 22.2 %all-to-all-start = ((bf16[32,32,256]{2,1,0:T(8,128)(2,1)}), bf16[32,32,256]{2,1,0:T(8,128)(2,1)S(1)}, u32[]{:S(2)}, u32[]{:S(2)}) async-start(bf16[32,32,256]{2,1,0:T(8,128)(2,1)} %bitcast.11), calls=%async_computation | async-start | bytes 1048576 | tf_op jit(solution)/shard_map/all_to_all | solution.py:208
  31.3 24.3 %all-to-all-start.1 = ((f32[16,1,128]{2,1,0:T(1,128)}), f32[16,1,128]{2,1,0:T(1,128)S(1)}, u32[]{:S(2)}, u32[]{:S(2)}) async-start(f32[16,1,128]{2,1,0:T(1,128)} %shard_map.68), calls=%async_computation.1 | async-start | bytes 16384 | tf_op jit(solution)/shard_map/all_to_all | solution.py:208
  56.8 14.8 %all-to-all-start.2 = ((f32[16,1,128]{2,1,0:T(1,128)}), f32[16,1,128]{2,1,0:T(1,128)S(1)}, u32[]{:S(2)}, u32[]{:S(2)}) async-start(f32[16,1,128]{2,1,0:T(1,128)} %get-tuple-element.6), calls=%async_computation.2 | async-start | bytes 16384 | tf_op jit(solution)/shard_map/all_to_all | solution.py:208
  72.4 14.0 %all-to-all-start.3 = ((f32[32,8,128]{2,1,0:T(8,128)}), f32[32,8,128]{2,1,0:T(8,128)S(1)}, u32[]{:S(2)}, u32[]{:S(2)}) async-start(f32[32,8,128]{2,1,0:T(8,128)} %shard_map.70), calls=%async_computation.3 | async-start | bytes 262144 | tf_op jit(solution)/shard_map/all_to_all | solution.py:208
  79.4 1.1 copy-start
  88.2 0.8 copy-start.1
Sparse Core Ops, SparseCore 0:
  10.1 89.5 all-gather.1

commit v6 on v5

--- a/solution.py
+++ b/solution.py
@@ -94,21 +94,17 @@
         out_ref[j] = tile
 
 
-def finish_rows(rows, at_ref, masses_ref, row_ref, out_ref):
+def finish_rows(rows, masses_ref, row_ref, out_ref):
     mass = masses_ref[0]
     for j in range(1, masses_ref.shape[0]):
         mass += masses_ref[j]
-    row = row_ref[...]
-    tile = jnp.concatenate([row[:3], mass, row[4:]], axis=0)
-    lane = lax.broadcasted_iota(jnp.int32, tile.shape, 1)
-    tile = jnp.where(lane < rows, tile, 0.0)
-    per = LANES // rows
-    placed = jnp.zeros_like(tile)
-    for k in range(per):
-        moved = pltpu.roll(tile, k * rows, 1) if k else tile
-        placed = jnp.where(at_ref[0] % per == k, moved, placed)
+    lane = lax.broadcasted_iota(jnp.int32, mass.shape, 1)
+    side = jnp.zeros_like(mass)
+    for k, row in enumerate([row_ref[0:1, :], row_ref[1:2, :], row_ref[2:3, :], mass]):
+        moved = pltpu.roll(row, k * rows, 1) if k else row
+        side = jnp.where(lane // rows == k, moved, side)
     for j in range(out_ref.shape[0]):
-        out_ref[j] = placed
+        out_ref[j] = side
 
 
 def owner_at(place, n_z):
@@ -132,16 +128,19 @@
     loss = [jnp.float32(0.0) for _ in range(loss_ref.shape[0])]
     lane = lax.broadcasted_iota(jnp.int32, (1, LANES), 1)
     for i in range(groups):
-        tile = jnp.zeros(rows_ref.shape[1:], F32)
         codes = jnp.zeros((1, LANES), jnp.int32)
+        stats = [jnp.ones((1, LANES), F32) for _ in range(4)]
         for k in range(per):
             j = owner_at(i * per + k, n_z)
-            tile += rows_ref[j]
+            for q in range(4):
+                shift = (k - q) * mine % LANES
+                part = pltpu.roll(rows_ref[j], shift, 1) if shift else rows_ref[j]
+                stats[q] = jnp.where(lane // mine == k, part, stats[q])
             code = codes_ref[j // per : j // per + 1, :]
             shift = (k - j % per) * mine % LANES
             code = pltpu.roll(code, shift, 1) if shift else code
             codes = jnp.where(lane // mine == k, code, codes)
-        peak, limit, target, mass = (tile[k : k + 1] for k in range(4))
+        peak, limit, target, mass = stats
         live = (codes & 1).astype(F32)
         rel = (codes >> 1) - at_ref[1]
         row_loss = live * (jnp.log(mass) + peak - target)
@@ -245,9 +244,8 @@
     )
     done = call(
         functools.partial(finish_rows, mine),
-        shape((n_plane, 8, LANES), F32),
+        shape((n_plane, 1, LANES), F32),
         rows * 16,
-        (at_plane % 2 * n_z + at_plane // 2).reshape(1),
         swap(masses, "z"),
         row_stats,
     )

time: 114 us -> 114 us (level)
  no operation moved by 1% of the time
where the time goes in v6:
time: 114 us; the launch traced here: 113 us
  waiting for transfers between devices  49.7 us (44%)
  starting transfers between devices  33.2 us (29%)
  between operations  14.1 us (12%)
  Pallas kernels  12.2 us (11%)
  local copies, waits for them, and re-layouts  3.45 us (3%)
    all_to_all x4, waiting for transfers between devices, swap(): return lax.all_to_all(parts, axis, split_axis=0, concat_axis=0, tiled=True)  37.5 us
    all_to_all x4, starting transfers between devices, swap(): return lax.all_to_all(parts, axis, split_axis=0, concat_axis=0, tiled=True)  33.2 us
    all_gather x1, waiting for transfers between devices, per_device(): whole = lax.all_gather(hidden, ('core', 'z'), axis=0, tiled=True)  11.5 us
    pallas_call x1, Pallas kernels, per_device(): pl.pallas_call(functools.partial(head_product, tile), in_specs=[any_space...  6.83 us
    pallas_call x5, Pallas kernels, call(): pl.pallas_call(kernel, out_shape=outs, in_specs=[SMEM if a.size < 8 else...  5.34 us
  transfers between devices with their start and end apart: 5, of which 5 were waited for; matrix products, arithmetic and copies ran while one was open for 2% of the time, Pallas kernels for 5%

profile of v6, /device:TPU:1, one launch (start us, length us, event | category | flops | bytes accessed | tf_op | source)
XLA Modules:
  0.0 113.4 jit_solution(13825023073442802488)
XLA Ops:
  7.2 0.0 all-gather.2.cloned.1.call-start
  7.2 0.7 all-gather.2.cloned.1.call-update
  7.9 10.4 %all-to-all-start = ((bf16[32,32,256]{2,1,0:T(8,128)(2,1)}), bf16[32,32,256]{2,1,0:T(8,128)(2,1)S(1)}, u32[]{:S(2)}, u32[]{:S(2)}) async-start(bf16[32,32,256]{2,1,0:T(8,128)(2,1)} %bitcast.10), calls=%async_computation | async-start | bytes 1048576 | tf_op jit(solution)/shard_map/all_to_all | solution.py:207
  18.3 0.8 dynamic_slice.7
  19.1 0.8 dynamic-slice_bitcast_fusion
  19.9 0.1 copy.7.teacher_ref
  20.0 10.1 %all-to-all-done.logits_ref = bf16[32,32,256]{2,1,0:T(8,128)(2,1)S(1)} async-done(((bf16[32,32,256]{2,1,0:T(8,128)(2,1)}), bf16[32,32,256]{2,1,0:T(8,128)(2,1)S(1)}, u32[]{:S(2)}, u32[]{:S(2)}) %all-to-all-start) | async-done | bytes 524320 | tf_op jit(solution)/shard_map/all_to_all | solution.py:207
  30.1 1.2 %shard_map.68 = f32[16,1,128]{2,1,0:T(1,128)} custom-call(s32[1]{0:T(128)} %bitcast.2.at_ref, bf16[32,32,256]{2,1,0:T(8,128)(2,1)S(1)} %all-to-all-done.logits_ref, s32[32,1]{1,0:T(8,128)S(1)} %copy.7.teacher_ref), custom_call_target="tpu_custom_call" | custom-call | flops 5242880 | bytes 532612 | tf_op jit(solution)/shard_map/pallas_call | solution.py:196
  31.3 13.0 %all-to-all-start.1 = ((f32[16,1,128]{2,1,0:T(1,128)}), f32[16,1,128]{2,1,0:T(1,128)S(1)}, u32[]{:S(2)}, u32[]{:S(2)}) async-start(f32[16,1,128]{2,1,0:T(1,128)} %shard_map.68), calls=%async_computation.1 | async-start | bytes 16384 | tf_op jit(solution)/shard_map/all_to_all | solution.py:207
  44.3 11.3 %all-to-all-done.1.parts_ref = f32[16,1,128]{2,1,0:T(1,128)S(1)} async-done(((f32[16,1,128]{2,1,0:T(1,128)}), f32[16,1,128]{2,1,0:T(1,128)S(1)}, u32[]{:S(2)}, u32[]{:S(2)}) %all-to-all-start.1) | async-done | bytes 8224 | tf_op jit(solution)/shard_map/all_to_all | solution.py:207
  55.6 1.3 %shard_map.69 = (f32[8,128]{1,0:T(8,128)S(1)}, f32[16,1,128]{2,1,0:T(1,128)}) custom-call(s32[1]{0:T(128)} %bitcast.2.at_ref, f32[16,1,128]{2,1,0:T(1,128)S(1)} %all-to-all-done.1.parts_ref, bf16[32,32,256]{2,1,0:T(8,128)(2,1)S(1)} %all-to-all-done.logits_ref, s32[32,1]{1,0:T(8,128)S(1)} %copy.7.teacher_ref, f32[1,128]{1,0:T(1,128)S(1)} %pad_bitcast_fusion.eta_ref), custom_call_target="tpu_custom_call" | custom-call | flops 5242880 | bytes 545412 | tf_op jit(solution)/shard_map/pallas_call | solution.py:196
  56.8 3.5 %all-to-all-start.2 = ((f32[16,1,128]{2,1,0:T(1,128)}), f32[16,1,128]{2,1,0:T(1,128)S(1)}, u32[]{:S(2)}, u32[]{:S(2)}) async-start(f32[16,1,128]{2,1,0:T(1,128)} %get-tuple-element.6), calls=%async_computation.2 | async-start | bytes 16384 | tf_op jit(solution)/shard_map/all_to_all | solution.py:207
  60.3 0.7 add_bitcast_fusion.codes_ref
  61.0 10.6 %all-to-all-done.2.masses_ref = f32[16,1,128]{2,1,0:T(1,128)S(1)} async-done(((f32[16,1,128]{2,1,0:T(1,128)}), f32[16,1,128]{2,1,0:T(1,128)S(1)}, u32[]{:S(2)}, u32[]{:S(2)}) %all-to-all-start.2) | async-done | bytes 8224 | tf_op jit(solution)/shard_map/all_to_all | solution.py:207
  71.6 0.7 shard_map.70
  72.3 6.3 %all-to-all-start.3 = ((f32[32,1,128]{2,1,0:T(1,128)}), f32[32,1,128]{2,1,0:T(1,128)S(1)}, u32[]{:S(2)}, u32[]{:S(2)}) async-start(f32[32,1,128]{2,1,0:T(1,128)} %shard_map.70), calls=%async_computation.3 | async-start | bytes 32768 | tf_op jit(solution)/shard_map/all_to_all | solution.py:207
  78.6 0.1 pad_add_fusion.at_ref
  78.7 0.0 copy-start
  78.7 1.0 copy-done
  79.7 0.2 shard_map.71.zt_ref
  79.9 5.5 %all-to-all-done.3.rows_ref = f32[32,1,128]{2,1,0:T(1,128)S(1)} async-done(((f32[32,1,128]{2,1,0:T(1,128)}), f32[32,1,128]{2,1,0:T(1,128)S(1)}, u32[]{:S(2)}, u32[]{:S(2)}) %all-to-all-start.3) | async-done | bytes 16416 | tf_op jit(solution)/shard_map/all_to_all | solution.py:207
  85.5 2.0 %shard_map.72 = (bf16[256,1024]{1,0:T(8,128)(2,1)S(1)}, f32[2]{0:T(128)}) custom-call(s32[2]{0:T(128)S(1)} %pad_add_fusion.at_ref, f32[32,1,128]{2,1,0:T(1,128)S(1)} %all-to-all-done.3.rows_ref, bf16[256,1024]{1,0:T(8,128)(2,1)S(1)} %shard_map.71.zt_ref, s32[8,128]{1,0:T(8,128)S(1)} %add_bitcast_fusion.codes_ref), custom_call_target="tpu_custom_call" | custom-call | flops 5242880 | bytes 1069072 | tf_op jit(solution)/shard_map/pallas_call | solution.py:196
  87.4 0.0 copy-start.1
  87.4 0.8 copy-done.1
  88.2 11.5 %all-gather.2.cloned.1.call-done.hidden_ref = bf16[1024,5376]{1,0:T(8,128)(2,1)} async-done(((bf16[32,5376]{1,0:T(8,128)(2,1)}), bf16[1024,5376]{1,0:T(8,128)(2,1)}) %all-gather.2.cloned.1.call-update) | async-done | bytes 11010064 | tf_op jit(solution)/shard_map/all_gather | solution.py:223
  99.7 6.8 %shard_map.73 = bf16[256,5376]{1,0:T(8,128)(2,1)} custom-call(bf16[256,1024]{1,0:T(8,128)(2,1)} %copy-done.1, bf16[1024,5376]{1,0:T(8,128)(2,1)} %all-gather.2.cloned.1.call-done.hidden_ref), custom_call_target="tpu_custom_call" | custom-call | flops 2818572288 | bytes 13762560 | tf_op jit(solution)/shard_map/pallas_call | solution.py:269
  (1 shorter events, 0.0 us)
Async XLA Ops:
  7.2 92.6 %all-gather.2.cloned.1.call-start = ((), (), s32[]{:S(2)}) async-start(), calls=%async_computation.4 | async-start | bytes 11354112 | tf_op jit(solution)/shard_map/all_gather | solution.py:223
  7.9 22.2 %all-to-all-start = ((bf16[32,32,256]{2,1,0:T(8,128)(2,1)}), bf16[32,32,256]{2,1,0:T(8,128)(2,1)S(1)}, u32[]{:S(2)}, u32[]{:S(2)}) async-start(bf16[32,32,256]{2,1,0:T(8,128)(2,1)} %bitcast.10), calls=%async_computation | async-start | bytes 1048576 | tf_op jit(solution)/shard_map/all_to_all | solution.py:207
  31.3 24.3 %all-to-all-start.1 = ((f32[16,1,128]{2,1,0:T(1,128)}), f32[16,1,128]{2,1,0:T(1,128)S(1)}, u32[]{:S(2)}, u32[]{:S(2)}) async-start(f32[16,1,128]{2,1,0:T(1,128)} %shard_map.68), calls=%async_computation.1 | async-start | bytes 16384 | tf_op jit(solution)/shard_map/all_to_all | solution.py:207
  56.8 14.8 %all-to-all-start.2 = ((f32[16,1,128]{2,1,0:T(1,128)}), f32[16,1,128]{2,1,0:T(1,128)S(1)}, u32[]{:S(2)}, u32[]{:S(2)}) async-start(f32[16,1,128]{2,1,0:T(1,128)} %get-tuple-element.6), calls=%async_computation.2 | async-start | bytes 16384 | tf_op jit(solution)/shard_map/all_to_all | solution.py:207
  72.3 13.2 %all-to-all-start.3 = ((f32[32,1,128]{2,1,0:T(1,128)}), f32[32,1,128]{2,1,0:T(1,128)S(1)}, u32[]{:S(2)}, u32[]{:S(2)}) async-start(f32[32,1,128]{2,1,0:T(1,128)} %shard_map.70), calls=%async_computation.3 | async-start | bytes 32768 | tf_op jit(solution)/shard_map/all_to_all | solution.py:207
  78.7 1.1 copy-start
  87.4 0.8 copy-start.1
Sparse Core Ops, SparseCore 0:
  10.1 89.5 all-gather.1

commit v7 on v6

--- a/solution.py
+++ b/solution.py
@@ -156,27 +156,24 @@
         loss_ref[k] = loss[k]
 
 
-def head_product(tile, grads_ref, hidden_ref, out_ref, weights, held, total, result, sems, out_sems):
+def head_product(tile, grads_ref, hidden_ref, out_ref, held, total, result, sems, out_sems):
     rows, width = hidden_ref.shape
     half = rows // 2
     lower, upper = pl.ds(0, half), pl.ds(half, half)
     first = pltpu.make_async_copy(hidden_ref.at[lower], held.at[lower], sems.at[0])
     second = pltpu.make_async_copy(hidden_ref.at[upper], held.at[upper], sems.at[1])
-    left = pltpu.make_async_copy(grads_ref, weights, sems.at[2])
-    left.start()
     first.start()
     second.start()
     starts = list(range(0, width, tile))
-    left.wait()
     first.wait()
     for s in starts:
         at = slice(s, min(s + tile, width))
-        total[:, at] = jnp.dot(weights[:, :half], held[:half, at], preferred_element_type=F32)
+        total[:, at] = jnp.dot(grads_ref[:, :half], held[:half, at], preferred_element_type=F32)
     second.wait()
     out = []
     for i, s in enumerate(starts):
         at = slice(s, min(s + tile, width))
-        more = jnp.dot(weights[:, half:], held[half:, at], preferred_element_type=F32)
+        more = jnp.dot(grads_ref[:, half:], held[half:, at], preferred_element_type=F32)
         result[:, at] = (total[:, at] + more).astype(result.dtype)
         part = pl.ds(s, min(tile, width - s))
         out.append(pltpu.make_async_copy(result.at[:, part], out_ref.at[:, part], out_sems.at[i]))
@@ -264,22 +261,21 @@
         out_specs=(VMEM, SMEM),
     )
 
-    tile = 768
+    tile = 512
     any_space = pl.BlockSpec(memory_space=pl.ANY)
     head_grad = pl.pallas_call(
         functools.partial(head_product, tile),
-        in_specs=[any_space, any_space],
+        in_specs=[VMEM, any_space],
         out_specs=any_space,
         out_shape=shape((wide, width), jnp.bfloat16),
         scratch_shapes=[
-            pltpu.VMEM((wide, rows), jnp.bfloat16),
             pltpu.VMEM((rows, width), jnp.bfloat16),
             pltpu.VMEM((wide, width), F32),
             pltpu.VMEM((wide, width), jnp.bfloat16),
-            pltpu.SemaphoreType.DMA((3,)),
+            pltpu.SemaphoreType.DMA((2,)),
             pltpu.SemaphoreType.DMA((-(-width // tile),)),
         ],
-        compiler_params=pltpu.CompilerParams(vmem_limit_bytes=56 << 20),
+        compiler_params=pltpu.CompilerParams(vmem_limit_bytes=44 << 20),
         cost_estimate=pl.CostEstimate(
             flops=2 * rows * wide * width,
             bytes_accessed=2 * (rows * width + wide * width),

time: 114 us -> 114 us (level)
  no operation moved by 1% of the time
where the time goes in v7:
time: 114 us; the launch traced here: 113 us
  waiting for transfers between devices  50.5 us (44%)
  starting transfers between devices  33.2 us (29%)
  between operations  14.1 us (12%)
  Pallas kernels  12 us (11%)
  local copies, waits for them, and re-layouts  2.67 us (2%)
    all_to_all x4, waiting for transfers between devices, swap(): return lax.all_to_all(parts, axis, split_axis=0, concat_axis=0, tiled=True)  37.5 us
    all_to_all x4, starting transfers between devices, swap(): return lax.all_to_all(parts, axis, split_axis=0, concat_axis=0, tiled=True)  33.2 us
    all_gather x1, waiting for transfers between devices, per_device(): whole = lax.all_gather(hidden, ('core', 'z'), axis=0, tiled=True)  12.3 us
    pallas_call x1, Pallas kernels, per_device(): pl.pallas_call(functools.partial(head_product, tile), in_specs=[VMEM, any...  6.63 us
    pallas_call x5, Pallas kernels, call(): pl.pallas_call(kernel, out_shape=outs, in_specs=[SMEM if a.size < 8 else...  5.34 us
  transfers between devices with their start and end apart: 5, of which 5 were waited for; matrix products, arithmetic and copies ran while one was open for 2% of the time, Pallas kernels for 5%

profile of v7, /device:TPU:1, one launch (start us, length us, event | category | flops | bytes accessed | tf_op | source)
XLA Modules:
  0.0 113.2 jit_solution(11959169796604454355)
XLA Ops:
  7.2 0.0 all-gather.2.cloned.1.call-start
  7.2 0.7 all-gather.2.cloned.1.call-update
  7.9 10.4 %all-to-all-start = ((bf16[32,32,256]{2,1,0:T(8,128)(2,1)}), bf16[32,32,256]{2,1,0:T(8,128)(2,1)S(1)}, u32[]{:S(2)}, u32[]{:S(2)}) async-start(bf16[32,32,256]{2,1,0:T(8,128)(2,1)} %bitcast.10), calls=%async_computation | async-start | bytes 1048576 | tf_op jit(solution)/shard_map/all_to_all | solution.py:204
  18.3 0.8 dynamic_slice.7
  19.1 0.8 dynamic-slice_bitcast_fusion
  19.9 0.1 copy.7.teacher_ref
  20.0 10.1 %all-to-all-done.logits_ref = bf16[32,32,256]{2,1,0:T(8,128)(2,1)S(1)} async-done(((bf16[32,32,256]{2,1,0:T(8,128)(2,1)}), bf16[32,32,256]{2,1,0:T(8,128)(2,1)S(1)}, u32[]{:S(2)}, u32[]{:S(2)}) %all-to-all-start) | async-done | bytes 524320 | tf_op jit(solution)/shard_map/all_to_all | solution.py:204
  30.1 1.2 %shard_map.68 = f32[16,1,128]{2,1,0:T(1,128)} custom-call(s32[1]{0:T(128)} %bitcast.2.at_ref, bf16[32,32,256]{2,1,0:T(8,128)(2,1)S(1)} %all-to-all-done.logits_ref, s32[32,1]{1,0:T(8,128)S(1)} %copy.7.teacher_ref), custom_call_target="tpu_custom_call" | custom-call | flops 5242880 | bytes 532612 | tf_op jit(solution)/shard_map/pallas_call | solution.py:193
  31.3 13.0 %all-to-all-start.1 = ((f32[16,1,128]{2,1,0:T(1,128)}), f32[16,1,128]{2,1,0:T(1,128)S(1)}, u32[]{:S(2)}, u32[]{:S(2)}) async-start(f32[16,1,128]{2,1,0:T(1,128)} %shard_map.68), calls=%async_computation.1 | async-start | bytes 16384 | tf_op jit(solution)/shard_map/all_to_all | solution.py:204
  44.3 11.3 %all-to-all-done.1.parts_ref = f32[16,1,128]{2,1,0:T(1,128)S(1)} async-done(((f32[16,1,128]{2,1,0:T(1,128)}), f32[16,1,128]{2,1,0:T(1,128)S(1)}, u32[]{:S(2)}, u32[]{:S(2)}) %all-to-all-start.1) | async-done | bytes 8224 | tf_op jit(solution)/shard_map/all_to_all | solution.py:204
  55.6 1.3 %shard_map.69 = (f32[8,128]{1,0:T(8,128)S(1)}, f32[16,1,128]{2,1,0:T(1,128)}) custom-call(s32[1]{0:T(128)} %bitcast.2.at_ref, f32[16,1,128]{2,1,0:T(1,128)S(1)} %all-to-all-done.1.parts_ref, bf16[32,32,256]{2,1,0:T(8,128)(2,1)S(1)} %all-to-all-done.logits_ref, s32[32,1]{1,0:T(8,128)S(1)} %copy.7.teacher_ref, f32[1,128]{1,0:T(1,128)S(1)} %pad_bitcast_fusion.eta_ref), custom_call_target="tpu_custom_call" | custom-call | flops 5242880 | bytes 545412 | tf_op jit(solution)/shard_map/pallas_call | solution.py:193
  56.8 3.5 %all-to-all-start.2 = ((f32[16,1,128]{2,1,0:T(1,128)}), f32[16,1,128]{2,1,0:T(1,128)S(1)}, u32[]{:S(2)}, u32[]{:S(2)}) async-start(f32[16,1,128]{2,1,0:T(1,128)} %get-tuple-element.6), calls=%async_computation.2 | async-start | bytes 16384 | tf_op jit(solution)/shard_map/all_to_all | solution.py:204
  60.3 0.7 add_bitcast_fusion.codes_ref
  61.0 10.6 %all-to-all-done.2.masses_ref = f32[16,1,128]{2,1,0:T(1,128)S(1)} async-done(((f32[16,1,128]{2,1,0:T(1,128)}), f32[16,1,128]{2,1,0:T(1,128)S(1)}, u32[]{:S(2)}, u32[]{:S(2)}) %all-to-all-start.2) | async-done | bytes 8224 | tf_op jit(solution)/shard_map/all_to_all | solution.py:204
  71.6 0.7 shard_map.70
  72.3 6.3 %all-to-all-start.3 = ((f32[32,1,128]{2,1,0:T(1,128)}), f32[32,1,128]{2,1,0:T(1,128)S(1)}, u32[]{:S(2)}, u32[]{:S(2)}) async-start(f32[32,1,128]{2,1,0:T(1,128)} %shard_map.70), calls=%async_computation.3 | async-start | bytes 32768 | tf_op jit(solution)/shard_map/all_to_all | solution.py:204
  78.6 0.1 pad_add_fusion.at_ref
  78.7 0.0 copy-start
  78.7 1.0 copy-done
  79.7 0.2 shard_map.71.zt_ref
  79.9 5.5 %all-to-all-done.3.rows_ref = f32[32,1,128]{2,1,0:T(1,128)S(1)} async-done(((f32[32,1,128]{2,1,0:T(1,128)}), f32[32,1,128]{2,1,0:T(1,128)S(1)}, u32[]{:S(2)}, u32[]{:S(2)}) %all-to-all-start.3) | async-done | bytes 16416 | tf_op jit(solution)/shard_map/all_to_all | solution.py:204
  85.5 2.0 %shard_map.72 = (bf16[256,1024]{1,0:T(8,128)(2,1)S(1)}, f32[2]{0:T(128)}) custom-call(s32[2]{0:T(128)S(1)} %pad_add_fusion.at_ref, f32[32,1,128]{2,1,0:T(1,128)S(1)} %all-to-all-done.3.rows_ref, bf16[256,1024]{1,0:T(8,128)(2,1)S(1)} %shard_map.71.zt_ref, s32[8,128]{1,0:T(8,128)S(1)} %add_bitcast_fusion.codes_ref), custom_call_target="tpu_custom_call" | custom-call | flops 5242880 | bytes 1069072 | tf_op jit(solution)/shard_map/pallas_call | solution.py:193
  87.4 12.3 %all-gather.2.cloned.1.call-done.hidden_ref = bf16[1024,5376]{1,0:T(8,128)(2,1)} async-done(((bf16[32,5376]{1,0:T(8,128)(2,1)}), bf16[1024,5376]{1,0:T(8,128)(2,1)}) %all-gather.2.cloned.1.call-update) | async-done | bytes 11010064 | tf_op jit(solution)/shard_map/all_gather | solution.py:220
  99.7 6.6 %shard_map.73 = bf16[256,5376]{1,0:T(8,128)(2,1)} custom-call(bf16[256,1024]{1,0:T(8,128)(2,1)S(1)} %get-tuple-element.8.grads_ref, bf16[1024,5376]{1,0:T(8,128)(2,1)} %all-gather.2.cloned.1.call-done.hidden_ref), custom_call_target="tpu_custom_call" | custom-call | flops 2818572288 | bytes 13762560 | tf_op jit(solution)/shard_map/pallas_call | solution.py:266
  (1 shorter events, 0.0 us)
Async XLA Ops:
  7.2 92.6 %all-gather.2.cloned.1.call-start = ((), (), s32[]{:S(2)}) async-start(), calls=%async_computation.4 | async-start | bytes 11354112 | tf_op jit(solution)/shard_map/all_gather | solution.py:220
  7.9 22.2 %all-to-all-start = ((bf16[32,32,256]{2,1,0:T(8,128)(2,1)}), bf16[32,32,256]{2,1,0:T(8,128)(2,1)S(1)}, u32[]{:S(2)}, u32[]{:S(2)}) async-start(bf16[32,32,256]{2,1,0:T(8,128)(2,1)} %bitcast.10), calls=%async_computation | async-start | bytes 1048576 | tf_op jit(solution)/shard_map/all_to_all | solution.py:204
  31.3 24.3 %all-to-all-start.1 = ((f32[16,1,128]{2,1,0:T(1,128)}), f32[16,1,128]{2,1,0:T(1,128)S(1)}, u32[]{:S(2)}, u32[]{:S(2)}) async-start(f32[16,1,128]{2,1,0:T(1,128)} %shard_map.68), calls=%async_computation.1 | async-start | bytes 16384 | tf_op jit(solution)/shard_map/all_to_all | solution.py:204
  56.8 14.8 %all-to-all-start.2 = ((f32[16,1,128]{2,1,0:T(1,128)}), f32[16,1,128]{2,1,0:T(1,128)S(1)}, u32[]{:S(2)}, u32[]{:S(2)}) async-start(f32[16,1,128]{2,1,0:T(1,128)} %get-tuple-element.6), calls=%async_computation.2 | async-start | bytes 16384 | tf_op jit(solution)/shard_map/all_to_all | solution.py:204
  72.3 13.2 %all-to-all-start.3 = ((f32[32,1,128]{2,1,0:T(1,128)}), f32[32,1,128]{2,1,0:T(1,128)S(1)}, u32[]{:S(2)}, u32[]{:S(2)}) async-start(f32[32,1,128]{2,1,0:T(1,128)} %shard_map.70), calls=%async_computation.3 | async-start | bytes 32768 | tf_op jit(solution)/shard_map/all_to_all | solution.py:204
  78.7 1.1 copy-start
Sparse Core Ops, SparseCore 0:
  10.1 89.5 all-gather.1

commit v8 on v7

--- a/solution.py
+++ b/solution.py
@@ -163,7 +163,7 @@
     first = pltpu.make_async_copy(hidden_ref.at[lower], held.at[lower], sems.at[0])
     second = pltpu.make_async_copy(hidden_ref.at[upper], held.at[upper], sems.at[1])
     first.start()
-    second.start()
+    second.start(priority=1)
     starts = list(range(0, width, tile))
     first.wait()
     for s in starts:

time: 114 us -> 114 us (level)
  no operation moved by 1% of the time
where the time goes in v8:
time: 114 us; the launch traced here: 113 us
  waiting for transfers between devices  50.5 us (44%)
  starting transfers between devices  33.2 us (29%)
  between operations  14.1 us (12%)
  Pallas kernels  12 us (11%)
  local copies, waits for them, and re-layouts  2.67 us (2%)
    all_to_all x4, waiting for transfers between devices, swap(): return lax.all_to_all(parts, axis, split_axis=0, concat_axis=0, tiled=True)  37.5 us
    all_to_all x4, starting transfers between devices, swap(): return lax.all_to_all(parts, axis, split_axis=0, concat_axis=0, tiled=True)  33.2 us
    all_gather x1, waiting for transfers between devices, per_device(): whole = lax.all_gather(hidden, ('core', 'z'), axis=0, tiled=True)  12.3 us
    pallas_call x1, Pallas kernels, per_device(): pl.pallas_call(functools.partial(head_product, tile), in_specs=[VMEM, any...  6.61 us
    pallas_call x5, Pallas kernels, call(): pl.pallas_call(kernel, out_shape=outs, in_specs=[SMEM if a.size < 8 else...  5.34 us
  transfers between devices with their start and end apart: 5, of which 5 were waited for; matrix products, arithmetic and copies ran while one was open for 2% of the time, Pallas kernels for 5%

profile of v8, /device:TPU:1, one launch (start us, length us, event | category | flops | bytes accessed | tf_op | source)
XLA Modules:
  0.0 113.2 jit_solution(10652785468424188041)
XLA Ops:
  7.2 0.0 all-gather.2.cloned.1.call-start
  7.2 0.7 all-gather.2.cloned.1.call-update
  7.9 10.4 %all-to-all-start = ((bf16[32,32,256]{2,1,0:T(8,128)(2,1)}), bf16[32,32,256]{2,1,0:T(8,128)(2,1)S(1)}, u32[]{:S(2)}, u32[]{:S(2)}) async-start(bf16[32,32,256]{2,1,0:T(8,128)(2,1)} %bitcast.10), calls=%async_computation | async-start | bytes 1048576 | tf_op jit(solution)/shard_map/all_to_all | solution.py:204
  18.3 0.8 dynamic_slice.7
  19.1 0.8 dynamic-slice_bitcast_fusion
  19.9 0.1 copy.7.teacher_ref
  20.0 10.1 %all-to-all-done.logits_ref = bf16[32,32,256]{2,1,0:T(8,128)(2,1)S(1)} async-done(((bf16[32,32,256]{2,1,0:T(8,128)(2,1)}), bf16[32,32,256]{2,1,0:T(8,128)(2,1)S(1)}, u32[]{:S(2)}, u32[]{:S(2)}) %all-to-all-start) | async-done | bytes 524320 | tf_op jit(solution)/shard_map/all_to_all | solution.py:204
  30.1 1.2 %shard_map.68 = f32[16,1,128]{2,1,0:T(1,128)} custom-call(s32[1]{0:T(128)} %bitcast.2.at_ref, bf16[32,32,256]{2,1,0:T(8,128)(2,1)S(1)} %all-to-all-done.logits_ref, s32[32,1]{1,0:T(8,128)S(1)} %copy.7.teacher_ref), custom_call_target="tpu_custom_call" | custom-call | flops 5242880 | bytes 532612 | tf_op jit(solution)/shard_map/pallas_call | solution.py:193
  31.3 13.0 %all-to-all-start.1 = ((f32[16,1,128]{2,1,0:T(1,128)}), f32[16,1,128]{2,1,0:T(1,128)S(1)}, u32[]{:S(2)}, u32[]{:S(2)}) async-start(f32[16,1,128]{2,1,0:T(1,128)} %shard_map.68), calls=%async_computation.1 | async-start | bytes 16384 | tf_op jit(solution)/shard_map/all_to_all | solution.py:204
  44.3 11.3 %all-to-all-done.1.parts_ref = f32[16,1,128]{2,1,0:T(1,128)S(1)} async-done(((f32[16,1,128]{2,1,0:T(1,128)}), f32[16,1,128]{2,1,0:T(1,128)S(1)}, u32[]{:S(2)}, u32[]{:S(2)}) %all-to-all-start.1) | async-done | bytes 8224 | tf_op jit(solution)/shard_map/all_to_all | solution.py:204
  55.6 1.3 %shard_map.69 = (f32[8,128]{1,0:T(8,128)S(1)}, f32[16,1,128]{2,1,0:T(1,128)}) custom-call(s32[1]{0:T(128)} %bitcast.2.at_ref, f32[16,1,128]{2,1,0:T(1,128)S(1)} %all-to-all-done.1.parts_ref, bf16[32,32,256]{2,1,0:T(8,128)(2,1)S(1)} %all-to-all-done.logits_ref, s32[32,1]{1,0:T(8,128)S(1)} %copy.7.teacher_ref, f32[1,128]{1,0:T(1,128)S(1)} %pad_bitcast_fusion.eta_ref), custom_call_target="tpu_custom_call" | custom-call | flops 5242880 | bytes 545412 | tf_op jit(solution)/shard_map/pallas_call | solution.py:193
  56.8 3.5 %all-to-all-start.2 = ((f32[16,1,128]{2,1,0:T(1,128)}), f32[16,1,128]{2,1,0:T(1,128)S(1)}, u32[]{:S(2)}, u32[]{:S(2)}) async-start(f32[16,1,128]{2,1,0:T(1,128)} %get-tuple-element.6), calls=%async_computation.2 | async-start | bytes 16384 | tf_op jit(solution)/shard_map/all_to_all | solution.py:204
  60.3 0.7 add_bitcast_fusion.codes_ref
  61.0 10.6 %all-to-all-done.2.masses_ref = f32[16,1,128]{2,1,0:T(1,128)S(1)} async-done(((f32[16,1,128]{2,1,0:T(1,128)}), f32[16,1,128]{2,1,0:T(1,128)S(1)}, u32[]{:S(2)}, u32[]{:S(2)}) %all-to-all-start.2) | async-done | bytes 8224 | tf_op jit(solution)/shard_map/all_to_all | solution.py:204
  71.6 0.7 shard_map.70
  72.3 6.3 %all-to-all-start.3 = ((f32[32,1,128]{2,1,0:T(1,128)}), f32[32,1,128]{2,1,0:T(1,128)S(1)}, u32[]{:S(2)}, u32[]{:S(2)}) async-start(f32[32,1,128]{2,1,0:T(1,128)} %shard_map.70), calls=%async_computation.3 | async-start | bytes 32768 | tf_op jit(solution)/shard_map/all_to_all | solution.py:204
  78.6 0.1 pad_add_fusion.at_ref
  78.7 0.0 copy-start
  78.7 1.0 copy-done
  79.7 0.2 shard_map.71.zt_ref
  79.9 5.5 %all-to-all-done.3.rows_ref = f32[32,1,128]{2,1,0:T(1,128)S(1)} async-done(((f32[32,1,128]{2,1,0:T(1,128)}), f32[32,1,128]{2,1,0:T(1,128)S(1)}, u32[]{:S(2)}, u32[]{:S(2)}) %all-to-all-start.3) | async-done | bytes 16416 | tf_op jit(solution)/shard_map/all_to_all | solution.py:204
  85.5 2.0 %shard_map.72 = (bf16[256,1024]{1,0:T(8,128)(2,1)S(1)}, f32[2]{0:T(128)}) custom-call(s32[2]{0:T(128)S(1)} %pad_add_fusion.at_ref, f32[32,1,128]{2,1,0:T(1,128)S(1)} %all-to-all-done.3.rows_ref, bf16[256,1024]{1,0:T(8,128)(2,1)S(1)} %shard_map.71.zt_ref, s32[8,128]{1,0:T(8,128)S(1)} %add_bitcast_fusion.codes_ref), custom_call_target="tpu_custom_call" | custom-call | flops 5242880 | bytes 1069072 | tf_op jit(solution)/shard_map/pallas_call | solution.py:193
  87.4 12.3 %all-gather.2.cloned.1.call-done.hidden_ref = bf16[1024,5376]{1,0:T(8,128)(2,1)} async-done(((bf16[32,5376]{1,0:T(8,128)(2,1)}), bf16[1024,5376]{1,0:T(8,128)(2,1)}) %all-gather.2.cloned.1.call-update) | async-done | bytes 11010064 | tf_op jit(solution)/shard_map/all_gather | solution.py:220
  99.7 6.6 %shard_map.73 = bf16[256,5376]{1,0:T(8,128)(2,1)} custom-call(bf16[256,1024]{1,0:T(8,128)(2,1)S(1)} %get-tuple-element.8.grads_ref, bf16[1024,5376]{1,0:T(8,128)(2,1)} %all-gather.2.cloned.1.call-done.hidden_ref), custom_call_target="tpu_custom_call" | custom-call | flops 2818572288 | bytes 13762560 | tf_op jit(solution)/shard_map/pallas_call | solution.py:266
  (1 shorter events, 0.0 us)
Async XLA Ops:
  7.2 92.6 %all-gather.2.cloned.1.call-start = ((), (), s32[]{:S(2)}) async-start(), calls=%async_computation.4 | async-start | bytes 11354112 | tf_op jit(solution)/shard_map/all_gather | solution.py:220
  7.9 22.2 %all-to-all-start = ((bf16[32,32,256]{2,1,0:T(8,128)(2,1)}), bf16[32,32,256]{2,1,0:T(8,128)(2,1)S(1)}, u32[]{:S(2)}, u32[]{:S(2)}) async-start(bf16[32,32,256]{2,1,0:T(8,128)(2,1)} %bitcast.10), calls=%async_computation | async-start | bytes 1048576 | tf_op jit(solution)/shard_map/all_to_all | solution.py:204
  31.3 24.3 %all-to-all-start.1 = ((f32[16,1,128]{2,1,0:T(1,128)}), f32[16,1,128]{2,1,0:T(1,128)S(1)}, u32[]{:S(2)}, u32[]{:S(2)}) async-start(f32[16,1,128]{2,1,0:T(1,128)} %shard_map.68), calls=%async_computation.1 | async-start | bytes 16384 | tf_op jit(solution)/shard_map/all_to_all | solution.py:204
  56.8 14.8 %all-to-all-start.2 = ((f32[16,1,128]{2,1,0:T(1,128)}), f32[16,1,128]{2,1,0:T(1,128)S(1)}, u32[]{:S(2)}, u32[]{:S(2)}) async-start(f32[16,1,128]{2,1,0:T(1,128)} %get-tuple-element.6), calls=%async_computation.2 | async-start | bytes 16384 | tf_op jit(solution)/shard_map/all_to_all | solution.py:204
  72.3 13.2 %all-to-all-start.3 = ((f32[32,1,128]{2,1,0:T(1,128)}), f32[32,1,128]{2,1,0:T(1,128)S(1)}, u32[]{:S(2)}, u32[]{:S(2)}) async-start(f32[32,1,128]{2,1,0:T(1,128)} %shard_map.70), calls=%async_computation.3 | async-start | bytes 32768 | tf_op jit(solution)/shard_map/all_to_all | solution.py:204
  78.7 1.1 copy-start
Sparse Core Ops, SparseCore 0:
  10.1 89.5 all-gather.1
